TPU v7x, 256 devices: a whole 4x4x8 slice. The times are simulated.
256 devices in a mesh: wl: 4 (over y), gz: 64 (over x, z, core).
Axes of the slice: x: 4, y: 4, z: 8, core: 2. Of those that a mesh axis runs over, the one named last changes fastest.
Arguments:
- source_fwd: float32 [4, 3, 64, 96, 128], P('wl', None, 'gz'), may hold values from -13 to 13
- source_adj: float32 [4, 3, 64, 96, 128], P('wl', None, 'gz'), may hold values from -13 to 13
- permittivity: float32 [3, 64, 96, 128], P(None, 'gz'), may hold values from 1 to 4
- omegas: float32 [4], P('wl'), may hold values from 0.15 to 0.45
- pml_widths: int32 [3], replicated, may hold values from 2 to 4
- design_mask: int32 [64], P('gz'), may hold values 0 or 1
Outputs:
- gradient: float32 [64, 96, 128], P('gz', 'wl')
All inputs are finite; a program needn't handle non-finite values. No bound on the sum of `design_mask` on one device may be relied on, other than what follows from the above.
Results may differ from a plain program's by a relative error of at most 0.0003.
Values sent between devices are 32-bit elements; how exact they have to be, the bound alone decides.
No kernel may reach another device: no remote copies, remote signals or barrier semaphores. Data moves between devices by JAX's collectives and lax.ppermute only.
A program may use at most 64 MiB of HBM per device.

v0:
```python
import jax
import jax.numpy as jnp
from jax import lax
from jax.sharding import PartitionSpec as P

ITERS = 3


SIGMA_MAX = 1.0


def passed_along(value, axis, by):
    size = lax.axis_size(axis)
    pairs = [(i, i + by) for i in range(size) if 0 <= i + by < size]
    return lax.ppermute(value, axis, pairs)


def profile(positions, length, layer_width, angular):
    width_f = layer_width.astype(jnp.float32)
    depth_cells = jnp.clip(
        jnp.maximum(width_f - positions, positions - (length - 1 - width_f)), 0.0, width_f
    )
    ratios = SIGMA_MAX * (depth_cells / width_f) ** 3 / angular[:, None]
    denominator = 1.0 + ratios * ratios
    return (1.0 / denominator, -ratios / denominator)


def shaped(factor, target):
    return (factor[0].reshape(target), factor[1].reshape(target))


def times_factor(factor, component):
    real_part = component[:, :, 0]
    imag_part = component[:, :, 1]
    return jnp.stack(
        [
            factor[0] * real_part - factor[1] * imag_part,
            factor[0] * imag_part + factor[1] * real_part,
        ],
        axis=2,
    )


def forward_diff(component, dim_index):
    extent = component.shape[dim_index]
    shifted = jnp.concatenate(
        [
            lax.slice_in_dim(component, 1, extent, axis=dim_index),
            jnp.zeros_like(lax.slice_in_dim(component, 0, 1, axis=dim_index)),
        ],
        axis=dim_index,
    )
    return shifted - component


def backward_diff(component, dim_index):
    extent = component.shape[dim_index]
    shifted = jnp.concatenate(
        [
            jnp.zeros_like(lax.slice_in_dim(component, 0, 1, axis=dim_index)),
            lax.slice_in_dim(component, 0, extent - 1, axis=dim_index),
        ],
        axis=dim_index,
    )
    return component - shifted


def plane_diff(component):
    return component[:, :, :, 1:] - component[:, :, :, :-1]


def curl_magnetic(magn_x, magn_y, magn_z, x_edge, y_edge, z_edge):
    inner_x = magn_x[:, :, :, 1:]
    inner_y = magn_y[:, :, :, 1:]
    curl_x = times_factor(y_edge, backward_diff(magn_z, 5)) - times_factor(
        z_edge, plane_diff(magn_y)
    )
    curl_y = times_factor(z_edge, plane_diff(magn_x)) - times_factor(
        x_edge, backward_diff(magn_z, 4)
    )
    curl_z = times_factor(x_edge, backward_diff(inner_y, 4)) - times_factor(
        y_edge, backward_diff(inner_x, 5)
    )
    return jnp.stack([curl_x, curl_y, curl_z], axis=3)


def bilinear(left, right):
    dims = (2, 3, 4, 5)
    left_re, left_im = (left[:, :, 0], left[:, :, 1])
    right_re, right_im = (right[:, :, 0], right[:, :, 1])
    return (
        jnp.sum(left_re * right_re - left_im * right_im, axis=dims),
        jnp.sum(left_re * right_im + left_im * right_re, axis=dims),
    )


def complex_div(upper, lower):
    denominator = lower[0] * lower[0] + lower[1] * lower[1]
    return (
        (upper[0] * lower[0] + upper[1] * lower[1]) / denominator,
        (upper[1] * lower[0] - upper[0] * lower[1]) / denominator,
    )


def scale_by(coefficient, fields):
    coef_re = coefficient[0][:, :, None, None, None, None]
    coef_im = coefficient[1][:, :, None, None, None, None]
    fields_re, fields_im = (fields[:, :, 0], fields[:, :, 1])
    return jnp.stack(
        [coef_re * fields_re - coef_im * fields_im, coef_re * fields_im + coef_im * fields_re],
        axis=2,
    )


def body(source_fwd, source_adj, permittivity, omegas, pml_widths, design_mask):
    slab_count = lax.axis_size("gz")
    slab_index = lax.axis_index("gz")
    wavecount = omegas.shape[0]
    planes, rows_x, rows_y = (source_fwd.shape[2], source_fwd.shape[3], source_fwd.shape[4])
    total_planes = planes * slab_count
    first_plane = (slab_index * planes).astype(jnp.float32)
    local_planes = jnp.arange(planes, dtype=jnp.float32) + first_plane
    pos_x = jnp.arange(rows_x, dtype=jnp.float32)
    pos_y = jnp.arange(rows_y, dtype=jnp.float32)
    x_half = shaped(
        profile(pos_x + 0.5, rows_x, pml_widths[0], omegas), (wavecount, 1, 1, rows_x, 1)
    )
    y_half = shaped(
        profile(pos_y + 0.5, rows_y, pml_widths[1], omegas), (wavecount, 1, 1, 1, rows_y)
    )
    x_edge = shaped(profile(pos_x, rows_x, pml_widths[0], omegas), (wavecount, 1, 1, rows_x, 1))
    y_edge = shaped(profile(pos_y, rows_y, pml_widths[1], omegas), (wavecount, 1, 1, 1, rows_y))
    z_edge = shaped(
        profile(local_planes, total_planes, pml_widths[2], omegas), (wavecount, 1, planes, 1, 1)
    )
    weight = (omegas * omegas).reshape(wavecount, 1, 1, 1, 1, 1, 1)
    material = permittivity[None, None, None] * weight
    z_half = shaped(
        profile(local_planes + 0.5, total_planes, pml_widths[2], omegas),
        (wavecount, 1, planes, 1, 1),
    )

    def apply_op(fields):
        upper = passed_along(fields[:, :, :, 0:2, 0:1], "gz", -1)
        elec_x, elec_y, elec_z = (fields[:, :, :, 0], fields[:, :, :, 1], fields[:, :, :, 2])
        reach_x = jnp.concatenate([elec_x, upper[:, :, :, 0]], axis=3)
        reach_y = jnp.concatenate([elec_y, upper[:, :, :, 1]], axis=3)
        magn_x = times_factor(y_half, forward_diff(elec_z, 5)) - times_factor(
            z_half, plane_diff(reach_y)
        )
        magn_y = times_factor(z_half, plane_diff(reach_x)) - times_factor(
            x_half, forward_diff(elec_z, 4)
        )
        magn_z = times_factor(x_half, forward_diff(elec_y, 4)) - times_factor(
            y_half, forward_diff(elec_x, 5)
        )
        lower = passed_along(jnp.stack([magn_x, magn_y], axis=3), "gz", 1)
        below_x = jnp.concatenate([lower[:, :, :, 0], magn_x], axis=3)
        below_y = jnp.concatenate([lower[:, :, :, 1], magn_y], axis=3)
        return curl_magnetic(below_x, below_y, magn_z, x_edge, y_edge, z_edge) - material * fields

    sources = jnp.stack([source_fwd, source_adj], axis=1)
    residual = jnp.stack([sources, jnp.zeros_like(sources)], axis=2)
    image = apply_op(residual)
    direction = residual
    pushed = image
    first_re, first_im = bilinear(residual, image)
    second_re, second_im = bilinear(pushed, pushed)
    first_re, first_im, second_re, second_im = lax.psum(
        (first_re, first_im, second_re, second_im), "gz"
    )
    rho_now = (first_re, first_im)
    gram = (second_re, second_im)
    solution = jnp.zeros_like(residual)
    for iteration in range(ITERS):
        step_size = complex_div(rho_now, gram)
        solution = solution + scale_by(step_size, direction)
        residual = residual - scale_by(step_size, pushed)
        if iteration + 1 < ITERS:
            image = apply_op(residual)
            rho_re, rho_im = bilinear(residual, image)
            rho_next = lax.psum((rho_re, rho_im), "gz")
            mix_ratio = complex_div(rho_next, rho_now)
            direction = residual + scale_by(mix_ratio, direction)
            pushed = image + scale_by(mix_ratio, pushed)
            gram_re, gram_im = bilinear(pushed, pushed)
            gram = lax.psum((gram_re, gram_im), "gz")
            rho_now = rho_next
    forward_re, forward_im = (solution[:, 0, 0], solution[:, 0, 1])
    adjoint_re, adjoint_im = (solution[:, 1, 0], solution[:, 1, 1])
    product = jnp.sum(forward_re * adjoint_re - forward_im * adjoint_im, axis=1)
    local_terms = jnp.sum((omegas * omegas)[:, None, None, None] * product, axis=0)
    local_terms = local_terms * design_mask.astype(jnp.float32)[:, None, None]
    total = lax.psum(local_terms, "wl")
    share_rows = rows_x // lax.axis_size("wl")
    return lax.dynamic_slice_in_dim(total, lax.axis_index("wl") * share_rows, share_rows, 1)


def solution(mesh):
    return jax.shard_map(
        body,
        mesh=mesh,
        in_specs=(
            P("wl", None, "gz", None, None),
            P("wl", None, "gz", None, None),
            P(None, "gz", None, None),
            P("wl"),
            P(),
            P("gz"),
        ),
        out_specs=P("gz", "wl", None),
        check_vma=False,
    )
```

profile of v0, /device:TPU:1, one launch (start us, length us, event | category | flops | bytes accessed | tf_op | source)
XLA Modules:
  0.0 708.9 jit_solution(12440238171565690487)
XLA Ops:
  0.0 1.0 fusion.34
  1.1 5.1 collective-permute-start
  11.9 1.9 collective-permute-start.1
  14.3 4.3 collective-permute-done.1
  20.4 127.9 %all-reduce.29 = (f32[1,2]{1,0:T(1,128)S(1)}, f32[1,2]{1,0:T(1,128)S(1)}, f32[1,2]{1,0:T(1,128)S(1)}, f32[1,2]{1,0:T(1,128)S(1)}) all-reduce(f32[1,2]{1,0:T(1,128)S(1)} %bitcast.478, f32[1,2]{1,0:T(1,128)S(1)} %bitcast.477, f32[1,2]{1,0:T(1,128)S(1)} %bitcast.479, f32[1,2]{1,0:T(1,128)S(1)} %bitcast.476), channel_id=1, replica_groups=mesh['wl'=4,'gz'=64] {'gz'}, use_global_device_ids=true, to_apply=%region_1.2 | all-reduce | flops 8 | bytes 64 | tf_op jit(solution)/shard_map/psum | solution.py:169
  149.7 2.1 collective-permute-start.2
  152.2 6.7 collective-permute-done.2
  161.4 1.9 collective-permute-start.3
  164.2 4.2 collective-permute-done.3
  168.4 1.0 fusion.16
  170.4 1.0 fusion.18
  172.1 121.3 %all-reduce.28 = (f32[1,2]{1,0:T(1,128)S(1)}, f32[1,2]{1,0:T(1,128)S(1)}) all-reduce(f32[1,2]{1,0:T(1,128)S(1)} %bitcast.481, f32[1,2]{1,0:T(1,128)S(1)} %bitcast.480), channel_id=1, replica_groups=mesh['wl'=4,'gz'=64] {'gz'}, use_global_device_ids=true, to_apply=%region_11.12 | all-reduce | flops 4 | bytes 32 | tf_op jit(solution)/shard_map/psum | solution.py:182
  293.4 1.1 multiply_subtract_fusion.5
  294.7 126.7 %all-reduce.27 = (f32[1,2]{1,0:T(1,128)S(1)}, f32[1,2]{1,0:T(1,128)S(1)}) all-reduce(f32[1,2]{1,0:T(1,128)S(1)} %bitcast.485, f32[1,2]{1,0:T(1,128)S(1)} %bitcast.484), channel_id=1, replica_groups=mesh['wl'=4,'gz'=64] {'gz'}, use_global_device_ids=true, to_apply=%region_15.16 | all-reduce | flops 4 | bytes 32 | tf_op jit(solution)/shard_map/psum | solution.py:187
  423.3 2.6 collective-permute-start.4
  426.5 1.0 subtract_bitcast_fusion
  427.8 4.6 collective-permute-done.4
  433.6 1.9 collective-permute-start.5
  435.8 4.4 collective-permute-done.5
  441.5 0.9 copy-done.3
  442.6 120.7 %all-reduce.26 = (f32[1,2]{1,0:T(1,128)S(1)}, f32[1,2]{1,0:T(1,128)S(1)}) all-reduce(f32[1,2]{1,0:T(1,128)S(1)} %bitcast.487, f32[1,2]{1,0:T(1,128)S(1)} %bitcast.486), channel_id=1, replica_groups=mesh['wl'=4,'gz'=64] {'gz'}, use_global_device_ids=true, to_apply=%region_17.18 | all-reduce | flops 4 | bytes 32 | tf_op jit(solution)/shard_map/psum | solution.py:182
  564.6 1.0 multiply_subtract_fusion.2
  565.9 127.2 %all-reduce.25 = (f32[1,2]{1,0:T(1,128)S(1)}, f32[1,2]{1,0:T(1,128)S(1)}) all-reduce(f32[1,2]{1,0:T(1,128)S(1)} %bitcast.483, f32[1,2]{1,0:T(1,128)S(1)} %bitcast.482), channel_id=1, replica_groups=mesh['wl'=4,'gz'=64] {'gz'}, use_global_device_ids=true, to_apply=%region_23.24 | all-reduce | flops 4 | bytes 32 | tf_op jit(solution)/shard_map/psum | solution.py:187
  694.5 13.9 %psum.103 = f32[1,96,128]{2,1,0:T(8,128)S(1)} all-reduce(f32[1,96,128]{2,1,0:T(8,128)S(1)} %multiply_bitcast_fusion.1), channel_id=1, replica_groups=mesh['wl'=4,'gz'=64] {'wl'}, use_global_device_ids=true, to_apply=%region_25.26 | all-reduce | flops 12288 | bytes 98304 | tf_op jit(solution)/shard_map/psum | solution.py:194
  (208 shorter events, 20.0 us)
Async XLA Ops:
  1.1 10.4 %collective-permute-start = (f32[1,2,2,2,1,96,128]{6,5,1,2,4,3,0:T(8,128)S(1)}, f32[1,2,2,2,1,96,128]{6,5,1,2,4,3,0:T(8,128)S(1)}, u32[]{:S(2)}, u32[]{:S(2)}) collective-permute-start(f32[1,2,2,2,1,96,128]{6,5,1,2,4,3,0:T(8,128)S(1)} %copy.145), channel_id=1, source_target_pairs={{1,0},{2,1},{3,2},{4,3},{5,4},{6,5},{7,6},{8,7},{9,8},{10,9},{11,1... | collective-permute-start | bytes 1179656 | tf_op jit(solution)/shard_map/ppermute | solution.py:15
  10.7 149.2 %copy-start.25 = (f32[128]{0:T(128)}, f32[128]{0:T(128)S(1)}, u32[]{:S(2)}) copy-start(f32[128]{0:T(128)S(1)} %get-tuple-element.223) | copy-start | bytes 1540
  10.7 149.2 %copy-start.27 = (f32[128]{0:T(128)}, f32[128]{0:T(128)S(1)}, u32[]{:S(2)}) copy-start(f32[128]{0:T(128)S(1)} %get-tuple-element.224) | copy-start | bytes 1540
  10.8 161.0 %copy-start.2 = (f32[3,96,128]{2,1,0:T(8,128)}, f32[3,96,128]{2,1,0:T(8,128)S(1)}, u32[]{:S(2)}) copy-start(f32[3,96,128]{2,1,0:T(8,128)S(1)} %multiply_bitcast_fusion) | copy-start | bytes 442372
  11.9 6.6 collective-permute-start.1
  13.9 157.8 %copy-start.21 = (f32[128]{0:T(128)}, f32[128]{0:T(128)S(1)}, u32[]{:S(2)}) copy-start(f32[128]{0:T(128)S(1)} %get-tuple-element.221) | copy-start | bytes 1540
  13.9 157.8 %copy-start.23 = (f32[128]{0:T(128)}, f32[128]{0:T(128)S(1)}, u32[]{:S(2)}) copy-start(f32[128]{0:T(128)S(1)} %get-tuple-element.222) | copy-start | bytes 1540
  149.7 9.1 %collective-permute-start.2 = (f32[1,2,2,2,1,96,128]{6,5,1,2,4,3,0:T(8,128)S(1)}, f32[1,2,2,2,1,96,128]{6,5,1,2,4,3,0:T(8,128)S(1)}, u32[]{:S(2)}, u32[]{:S(2)}) collective-permute-start(f32[1,2,2,2,1,96,128]{6,5,1,2,4,3,0:T(8,128)S(1)} %copy.149), channel_id=1, source_target_pairs={{1,0},{2,1},{3,2},{4,3},{5,4},{6,5},{7,6},{8,7},{9,8},{10,9},{11,1... | collective-permute-start | bytes 1179656 | tf_op jit(solution)/shard_map/ppermute | solution.py:15
  158.9 1.1 copy-start.9
  158.9 1.1 copy-start.11
  159.0 1.0 copy-start.13
  159.1 1.0 copy-start.15
  161.4 6.9 collective-permute-start.3
  164.0 4.3 copy-start.10
  164.0 4.3 copy-start.12
  169.3 1.0 copy-start.19
  293.4 128.0 %copy-start.38 = (f32[1,2]{1,0:T(1,128)}, f32[1,2]{1,0:T(1,128)S(1)}, u32[]{:S(2)}) copy-start(f32[1,2]{1,0:T(1,128)S(1)} %get-tuple-element.25) | copy-start | bytes 28
  293.4 128.0 %copy-start.40 = (f32[1,2]{1,0:T(1,128)}, f32[1,2]{1,0:T(1,128)S(1)}, u32[]{:S(2)}) copy-start(f32[1,2]{1,0:T(1,128)S(1)} %get-tuple-element.26) | copy-start | bytes 28
  422.0 1.0 copy-start.5
  423.2 2.6 copy-start.43
  423.3 9.1 %collective-permute-start.4 = (f32[1,2,2,2,1,96,128]{6,5,1,2,4,3,0:T(8,128)S(1)}, f32[1,2,2,2,1,96,128]{6,5,1,2,4,3,0:T(8,128)S(1)}, u32[]{:S(2)}, u32[]{:S(2)}) collective-permute-start(f32[1,2,2,2,1,96,128]{6,5,1,2,4,3,0:T(8,128)S(1)} %copy.153), channel_id=1, source_target_pairs={{1,0},{2,1},{3,2},{4,3},{5,4},{6,5},{7,6},{8,7},{9,8},{10,9},{11,1... | collective-permute-start | bytes 1179656 | tf_op jit(solution)/shard_map/ppermute | solution.py:15
  433.6 6.6 collective-permute-start.5
  565.7 127.4 %copy-start.8 = (f32[1,2,1,3,1,96,128]{6,5,3,1,4,2,0:T(8,128)S(1)}, f32[1,2,1,3,1,96,128]{6,5,3,1,4,2,0:T(8,128)}, u32[]{:S(2)}) copy-start(f32[1,2,1,3,1,96,128]{6,5,3,1,4,2,0:T(8,128)} %get-tuple-element.193) | copy-start | bytes 884740
  693.3 1.0 copy-start.7
  (26 other events, 19.0 us)
where the time goes:
time: 711 us; the launch traced here: 709 us
  blocking collectives  638 us (90%)
  waiting for transfers between devices  24.8 us (3%)
  starting transfers between devices  15.5 us (2%)
  other arithmetic  13.1 us (2%)
  local copies, waits for them, and re-layouts  13.1 us (2%)
    psum x2, blocking collectives, body(): gram = lax.psum((gram_re, gram_im), 'gz')  254 us
    psum x2, blocking collectives, body(): rho_next = lax.psum((rho_re, rho_im), 'gz')  242 us
    psum x1, blocking collectives, body(): lax.psum((first_re, first_im, second_re, second_im), 'gz')  128 us
    ppermute x6, waiting for transfers between devices, passed_along(): return lax.ppermute(value, axis, pairs)  24.8 us
    ppermute x6, starting transfers between devices, passed_along(): return lax.ppermute(value, axis, pairs)  15.5 us
  transfers between devices with their start and end apart: 6, of which 6 were waited for; matrix products, arithmetic and copies ran while one was open for 0% of the time, Pallas kernels for 0%

commit v1 on v0

v1 whole, which is shorter than its diff:
```python
import jax
import jax.numpy as jnp
from jax import lax
from jax.experimental import pallas as pl
from jax.experimental.pallas import tpu as pltpu
from jax.sharding import PartitionSpec as P

SIGMA_MAX = 1.0
SHIFT = (0.0, 6.0, 12.0)
ROWS = 8
LANES = 128
GRAM = [(0, 0), (0, 1), (1, 1), (0, 2), (1, 2), (2, 2), (0, 3), (1, 3), (2, 3), (3, 3)]
PRODUCTS = [(i, j) for i in range(3) for j in range(3)]
VM = pltpu.VMEM


def cmul(a, b):
    return a[0] * b[0] - a[1] * b[1], a[0] * b[1] + a[1] * b[0]


def cadd(a, b):
    return a[0] + b[0], a[1] + b[1]


def csub(a, b):
    return a[0] - b[0], a[1] - b[1]


def cdiv(upper, lower):
    den = lower[0] * lower[0] + lower[1] * lower[1]
    return (
        (upper[0] * lower[0] + upper[1] * lower[1]) / den,
        (upper[1] * lower[0] - upper[0] * lower[1]) / den,
    )


def rowids():
    return lax.broadcasted_iota(jnp.int32, (ROWS, LANES), 0)


def laneids():
    return lax.broadcasted_iota(jnp.int32, (ROWS, LANES), 1)


class Shifts:
    def __init__(self):
        self.first_row = rowids() == 0
        self.last_row = rowids() == ROWS - 1
        self.first_lane = laneids() == 0
        self.last_lane = laneids() == LANES - 1

    def x_next(self, cur, nxt):
        return pltpu.roll(jnp.where(self.first_row, nxt, cur), ROWS - 1, 0)

    def x_prev(self, cur, prv):
        return pltpu.roll(jnp.where(self.last_row, prv, cur), 1, 0)

    def y_next(self, cur):
        return jnp.where(self.last_lane, 0.0, pltpu.roll(cur, LANES - 1, 1))

    def y_prev(self, cur):
        return jnp.where(self.first_lane, 0.0, pltpu.roll(cur, 1, 1))


def profile(positions, length, width, angular):
    depth = jnp.clip(jnp.maximum(width - positions, positions - (length - 1 - width)), 0.0, width)
    part = depth / width
    ratios = SIGMA_MAX * (part * part * part) / angular
    denominator = 1.0 + ratios * ratios
    return 1.0 / denominator, -ratios / denominator


def factor_kernel(total_planes, rows_x, widths, omegas, mask, place, fx, fv):
    angular = omegas[0]
    wx = widths[0].astype(jnp.float32)
    wy = widths[1].astype(jnp.float32)
    wz = widths[2].astype(jnp.float32)
    slab = place[0]
    for s in range(rows_x // ROWS):
        pos = (rowids() + s * ROWS).astype(jnp.float32)
        at = pl.ds(s * ROWS, ROWS)
        fx[0, at, :], fx[1, at, :] = profile(pos + 0.5, rows_x, wx, angular)
        fx[2, at, :], fx[3, at, :] = profile(pos, rows_x, wx, angular)
    pos = laneids().astype(jnp.float32)
    fv[0], fv[1] = profile(pos + 0.5, LANES, wy, angular)
    fv[2], fv[3] = profile(pos, LANES, wy, angular)
    plane = jnp.broadcast_to(slab.astype(jnp.float32), (ROWS, LANES))
    fv[4], fv[5] = profile(plane + 0.5, total_planes, wz, angular)
    fv[6], fv[7] = profile(plane, total_planes, wz, angular)
    below_re, below_im = profile(plane - 0.5, total_planes, wz, angular)
    inside = plane > 0.0
    fv[8] = jnp.where(inside, below_re, 0.0)
    fv[9] = jnp.where(inside, below_im, 0.0)
    fv[10] = jnp.broadcast_to(angular * angular, (ROWS, LANES))
    fv[11] = jnp.broadcast_to((slab % 2).astype(jnp.float32), (ROWS, LANES))
    fv[12] = jnp.broadcast_to(mask[0].astype(jnp.float32), (ROWS, LANES))


class Factors:
    def __init__(self, fv, fx):
        self.yh = (fv[0], fv[1])
        self.ye = (fv[2], fv[3])
        self.zh = (fv[4], fv[5])
        self.ze = (fv[6], fv[7])
        self.zb = (fv[8], fv[9])
        self.weight = fv[10]
        self.upper_core = fv[11] > 0.5
        self.fx = fx

    def x(self, s):
        at = pl.ds(s * ROWS, ROWS)
        return (self.fx[0, at, :], self.fx[1, at, :]), (self.fx[2, at, :], self.fx[3, at, :])


ZERO = 0.0


def zeros():
    return jnp.zeros((ROWS, LANES), jnp.float32)


def rmul(factor, real):
    return factor[0] * real, factor[1] * real


def curl_of(fac, sh, xe, hx, hy, hz, hx_b, hy_b, before):
    hy_p, hz_p = before
    dby = lambda h: tuple(p - sh.y_prev(p) for p in h)
    dbx = lambda h, q: tuple(p - sh.x_prev(p, r) for p, r in zip(h, q))
    cx = csub(cmul(fac.ye, dby(hz)), cmul(fac.ze, csub(hy, hy_b)))
    cy = csub(cmul(fac.ze, csub(hx, hx_b)), cmul(xe, dbx(hz, hz_p)))
    cz = csub(cmul(xe, dbx(hy, hy_p)), cmul(fac.ye, dby(hx)))
    return cx, cy, cz


def first_apply(fac, sh, b, rc, rz, eps, q, s, strips, before):
    at = pl.ds(s * ROWS, ROWS)
    after = pl.ds((s + 1) * ROWS, ROWS)
    last = s + 1 == strips
    core = fac.upper_core

    def up(c):
        return jnp.where(core, rz[q, c, at, :], rc[q, c, at, :])

    def dn(c, where):
        return jnp.where(core, rc[q, c, where, :], rz[q, c, where, :])

    ex, ey, ez = (b[q, c, at, :] for c in range(3))
    nxt = lambda c: zeros() if last else b[q, c, after, :]
    xh, xe = fac.x(s)
    dx_ez = sh.x_next(ez, nxt(2)) - ez
    dx_ey = sh.x_next(ey, nxt(1)) - ey
    dy_ez = sh.y_next(ez) - ez
    dy_ex = sh.y_next(ex) - ex
    hx = csub(rmul(fac.yh, dy_ez), rmul(fac.zh, up(1) - ey))
    hy = csub(rmul(fac.zh, up(0) - ex), rmul(xh, dx_ez))
    hz = csub(rmul(xh, dx_ey), rmul(fac.yh, dy_ex))
    bx, by, bz = (dn(c, at) for c in range(3))
    dx_bz = sh.x_next(bz, zeros() if last else dn(2, after)) - bz
    dy_bz = sh.y_next(bz) - bz
    hx_b = csub(rmul(fac.yh, dy_bz), rmul(fac.zb, ey - by))
    hy_b = csub(rmul(fac.zb, ex - bx), rmul(xh, dx_bz))
    curls = curl_of(fac, sh, xe, hx, hy, hz, hx_b, hy_b, before)
    out = []
    for c, e in enumerate((ex, ey, ez)):
        out.append((curls[c][0] - fac.weight * eps[c, at, :] * e, curls[c][1]))
    return out, (hy, hz)


def next_apply(fac, sh, exy, ez_ref, rc, rz, eps, q, s, strips, before, shift):
    at = pl.ds(s * ROWS, ROWS)
    after = pl.ds((s + 1) * ROWS, ROWS)
    last = s + 1 == strips
    core = fac.upper_core
    up = lambda c: tuple(jnp.where(core, rz[c, q, p, at, :], rc[c, q, p, at, :]) for p in range(2))
    dn = lambda c: tuple(jnp.where(core, rc[c, q, p, at, :], rz[c, q, p, at, :]) for p in range(2))
    ex = tuple(exy[0, q, p, at, :] for p in range(2))
    ey = tuple(exy[1, q, p, at, :] for p in range(2))
    ez = tuple(ez_ref[q, p, at, :] for p in range(2))
    ey_n = tuple(zeros() if last else exy[1, q, p, after, :] for p in range(2))
    ez_n = tuple(zeros() if last else ez_ref[q, p, after, :] for p in range(2))
    xh, xe = fac.x(s)
    dfx = lambda v, n: tuple(sh.x_next(a, b) - a for a, b in zip(v, n))
    dfy = lambda v: tuple(sh.y_next(a) - a for a in v)
    hx = csub(cmul(fac.yh, dfy(ez)), cmul(fac.zh, csub(up(1), ey)))
    hy = csub(cmul(fac.zh, csub(up(0), ex)), cmul(xh, dfx(ez, ez_n)))
    hz = csub(cmul(xh, dfx(ey, ey_n)), cmul(fac.yh, dfy(ex)))
    hx_b = csub(dn(0), cmul(fac.zb, ey))
    hy_b = cadd(dn(1), cmul(fac.zb, ex))
    curls = curl_of(fac, sh, xe, hx, hy, hz, hx_b, hy_b, before)
    out = []
    for c, e in enumerate((ex, ey, ez)):
        diagonal = fac.weight * eps[c, at, :] + shift
        out.append(tuple(curls[c][p] - diagonal * e[p] for p in range(2)))
    return out, (hy, hz)


def store_field(fac, sh, field, q, s, strips, held, uxy, uz, sc, sz):
    at = pl.ds(s * ROWS, ROWS)
    for c in range(2):
        for p in range(2):
            uxy[c, q, p, at, :] = field[c][p]
    for p in range(2):
        uz[q, p, at, :] = field[2][p]
    if held is not None:
        store_sends(fac, sh, held, field[2], q, s - 1, sc, sz)
    if s + 1 == strips:
        store_sends(fac, sh, field, (zeros(), zeros()), q, s, sc, sz)


def store_sends(fac, sh, field, ez_n, q, s, sc, sz):
    at = pl.ds(s * ROWS, ROWS)
    xh, _ = fac.x(s)
    ex, ey, ez = field
    dx_ez = tuple(sh.x_next(a, b) - a for a, b in zip(ez, ez_n))
    dy_ez = tuple(sh.y_next(a) - a for a in ez)
    part_x = cadd(cmul(fac.yh, dy_ez), cmul(fac.zh, ey))
    part_y = cadd(cmul(fac.zh, ex), cmul(xh, dx_ez))
    part_y = (-part_y[0], -part_y[1])
    for c, (down, above) in enumerate(((ex, part_x), (ey, part_y))):
        for p in range(2):
            sc[c, q, p, at, :] = jnp.where(fac.upper_core, down[p], above[p])
            sz[c, q, p, at, :] = jnp.where(fac.upper_core, above[p], down[p])


def first_kernel(strips, b, rc, rz, eps, fx, fv, uxy, uz, sc, sz):
    fac, sh = Factors(fv, fx), Shifts()
    for q in range(2):
        nil = (zeros(), zeros())
        before, held = (nil, nil), None
        for s in range(strips):
            field, before = first_apply(fac, sh, b, rc, rz, eps, q, s, strips, before)
            store_field(fac, sh, field, q, s, strips, held, uxy, uz, sc, sz)
            held = field


def second_kernel(strips, exy, ez, rc, rz, eps, fx, fv, uxy, uz, sc, sz):
    fac, sh = Factors(fv, fx), Shifts()
    for q in range(2):
        nil = (zeros(), zeros())
        before, held = (nil, nil), None
        for s in range(strips):
            field, before = next_apply(
                fac, sh, exy, ez, rc, rz, eps, q, s, strips, before, SHIFT[1]
            )
            store_field(fac, sh, field, q, s, strips, held, uxy, uz, sc, sz)
            held = field


def strip_of(uxy, uz, q, s):
    at = pl.ds(s * ROWS, ROWS)
    return [tuple(uxy[c, q, p, at, :] for p in range(2)) for c in range(2)] + [
        tuple(uz[q, p, at, :] for p in range(2))
    ]


def source_of(b, q, s):
    at = pl.ds(s * ROWS, ROWS)
    return [(b[q, c, at, :],) for c in range(3)]


def times(a, b):
    if len(a) == 1 and len(b) == 1:
        return (a[0] * b[0],)
    if len(a) == 1:
        return a[0] * b[0], a[0] * b[1]
    if len(b) == 1:
        return a[0] * b[0], a[1] * b[0]
    return cmul(a, b)


def dot_strip(left, right):
    total = None
    for a, b in zip(left, right):
        term = times(a, b)
        total = term if total is None else tuple(x + y for x, y in zip(total, term))
    return total


def gather_sums(sums):
    lane = lax.broadcasted_iota(jnp.int32, (1, LANES), 1)
    row = jnp.zeros((1, LANES), jnp.float32)
    for (g, q, p), block in sums.items():
        folded = jnp.sum(block, axis=0, keepdims=True)
        whole = jnp.sum(folded, axis=1, keepdims=True)
        row = jnp.where(lane == 4 * g + 2 * p + q, whole, row)
    return row


def add_sums(sums, g, q, term):
    for p, block in enumerate(term):
        key = (g, q, p)
        sums[key] = block if key not in sums else sums[key] + block


def sums_kernel(strips, b, uxy, uz, row):
    sums = {}
    for q in range(2):
        for s in range(strips):
            u = [source_of(b, q, s), strip_of(uxy, uz, q, s)]
            for g, (i, j) in enumerate(GRAM):
                if j < 2:
                    add_sums(sums, g, q, dot_strip(u[i], u[j]))
    row[...] = gather_sums(sums)


def products_kernel(strips, before, b, u1xy, u1z, u2xy, u2z, row, products):
    sums = {}
    for s in range(strips):
        at = pl.ds(s * ROWS, ROWS)
        both = []
        for q in range(2):
            u = [source_of(b, q, s), strip_of(u1xy, u1z, q, s), strip_of(u2xy, u2z, q, s)]
            both.append(u)
            for g, (i, j) in enumerate(GRAM):
                if j == 2:
                    add_sums(sums, g, q, dot_strip(u[i], u[j]))
        place = 0
        for i, j in PRODUCTS:
            for part in dot_strip(both[0][i], both[1][j]):
                products[place, at, :] = part
                place += 1
    row[...] = before[...] + gather_sums(sums)


def third_kernel(strips, before, b, u1xy, u1z, u2xy, u2z, rc, rz, eps, fx, fv, row):
    fac, sh = Factors(fv, fx), Shifts()
    sums = {}
    for q in range(2):
        nil = (zeros(), zeros())
        prior = (nil, nil)
        for s in range(strips):
            u3, prior = next_apply(
                fac, sh, u2xy, u2z, rc, rz, eps, q, s, strips, prior, SHIFT[2]
            )
            u = [source_of(b, q, s), strip_of(u1xy, u1z, q, s), strip_of(u2xy, u2z, q, s), u3]
            for g, (i, j) in enumerate(GRAM):
                if j == 3:
                    add_sums(sums, g, q, dot_strip(u[i], u[j]))
    row[...] = jnp.broadcast_to(before[...] + gather_sums(sums), row.shape)


def coefficients(gram):
    def image_of(v):
        out = [None] * 4
        for i, value in enumerate(v):
            if value is None:
                continue
            out[i + 1] = value if out[i + 1] is None else cadd(out[i + 1], value)
            if SHIFT[i] != 0.0:
                moved = (SHIFT[i] * value[0], SHIFT[i] * value[1])
                out[i] = moved if out[i] is None else cadd(out[i], moved)
        return out

    def plus(a, b):
        if a is None:
            return b
        return a if b is None else cadd(a, b)

    def minus(a, b):
        if b is None:
            return a
        return (-b[0], -b[1]) if a is None else csub(a, b)

    def scaled(factor, v):
        return [None if x is None else cmul(factor, x) for x in v]

    def form(left, right):
        total = None
        for i, a in enumerate(left):
            if a is None:
                continue
            inner = None
            for j, b in enumerate(right):
                if b is not None:
                    inner = plus(inner, cmul(b, gram[min(i, j), max(i, j)]))
            total = plus(total, cmul(a, inner))
        return total

    one = jnp.ones_like(gram[0, 0][0])
    residual = [(one, jnp.zeros_like(one)), None, None, None]
    image = [None, (one, jnp.zeros_like(one)), None, None]
    direction, pushed = residual, image
    rho, size = gram[0, 1], gram[1, 1]
    solution = [None] * 4
    for iteration in range(3):
        step = cdiv(rho, size)
        solution = [plus(a, b) for a, b in zip(solution, scaled(step, direction))]
        if iteration == 2:
            break
        residual = [minus(a, b) for a, b in zip(residual, scaled(step, pushed))]
        image = image_of(residual[:3])
        rho_next = form(residual, image)
        ratio = cdiv(rho_next, rho)
        direction = [plus(a, b) for a, b in zip(residual, scaled(ratio, direction))]
        pushed = [plus(a, b) for a, b in zip(image, scaled(ratio, pushed))]
        size = form(pushed, pushed)
        rho = rho_next
    return solution[:3]


def gradient_kernel(strips, rows, products, fv, out):
    total = jnp.sum(rows[...], axis=0, keepdims=True)
    lane, sub = laneids(), rowids()
    spread = jnp.broadcast_to(total, (ROWS, LANES))
    gram = {}
    for g, pair in enumerate(GRAM):
        parts = []
        for p in range(2):
            mine = lane == 4 * g + 2 * p + sub
            picked = jnp.sum(jnp.where(mine, spread, 0.0), axis=1, keepdims=True)
            parts.append(jnp.broadcast_to(picked, (ROWS, LANES)))
        gram[pair] = tuple(parts)
    coefs = coefficients(gram)
    scale = fv[10] * fv[12]
    one_row = lambda v, q: jnp.broadcast_to(v[q : q + 1, :], (ROWS, LANES))
    weights = []
    for i, j in PRODUCTS:
        left = tuple(one_row(x, 0) for x in coefs[i])
        right = tuple(one_row(x, 1) for x in coefs[j])
        both = cmul(left, right)
        weights.append(both[0] * scale)
        if (i, j) != (0, 0):
            weights.append(-both[1] * scale)
    per_share = strips // out.shape[0]
    for s in range(strips):
        at = pl.ds(s * ROWS, ROWS)
        value = None
        for place, weight in enumerate(weights):
            term = weight * products[place, at, :]
            value = term if value is None else value + term
        out[s // per_share, pl.ds((s % per_share) * ROWS, ROWS), :] = value


def call(kernel, outs, *args, smem=0, name=None, flops=0):
    specs = [pl.BlockSpec(memory_space=pltpu.SMEM if i < smem else VM) for i in range(len(args))]
    shapes = [jax.ShapeDtypeStruct(s, jnp.float32) for s in outs]
    outs_spec = [pl.BlockSpec(memory_space=VM) for _ in outs]
    nbytes = sum(4 * a.size for a in args)
    return pl.pallas_call(
        kernel,
        out_shape=shapes,
        in_specs=specs,
        out_specs=outs_spec,
        name=name,
        cost_estimate=pl.CostEstimate(flops=flops, bytes_accessed=nbytes, transcendentals=0),
        compiler_params=pltpu.CompilerParams(vmem_limit_bytes=32 * 1024 * 1024),
    )(*args)


def partial(fn, *args):
    def inner(*refs):
        fn(*args, *refs)

    return inner


def body(source_fwd, source_adj, permittivity, omegas, pml_widths, design_mask):
    slabs = lax.axis_size("gz")
    shares = lax.axis_size("wl")
    rows_x, rows_y = source_fwd.shape[3], source_fwd.shape[4]
    strips = rows_x // ROWS
    core_pairs = [(i, i ^ 1) for i in range(slabs)]
    chip_pairs = []
    for i in range(1, slabs - 1, 2):
        chip_pairs += [(i, i + 1), (i + 1, i)]
    place = lax.axis_index("gz").astype(jnp.int32).reshape(1)
    b = jnp.concatenate([source_fwd, source_adj], axis=0).reshape(2, 3, rows_x, rows_y)
    eps = permittivity.reshape(3, rows_x, rows_y)
    field = (2, 2, 2, rows_x, rows_y)
    plain = (2, 2, rows_x, rows_y)

    def swap(to_chip, to_core):
        from_chip = lax.ppermute(to_chip, "gz", chip_pairs)
        from_core = lax.ppermute(to_core, "gz", core_pairs)
        return from_core, from_chip

    rc, rz = swap(b, b)
    fx, fv = call(
        partial(factor_kernel, slabs, rows_x),
        [(4, rows_x, rows_y), (13, ROWS, LANES)],
        pml_widths,
        omegas,
        design_mask,
        place,
        smem=4,
        name="factors",
    )
    u1xy, u1z, sc, sz = call(
        partial(first_kernel, strips),
        [field, plain, field, field],
        b,
        rc,
        rz,
        eps,
        fx,
        fv,
        name="apply_first",
    )
    rc, rz = swap(sz, sc)
    (row,) = call(partial(sums_kernel, strips), [(1, LANES)], b, u1xy, u1z, name="sums")
    u2xy, u2z, sc, sz = call(
        partial(second_kernel, strips),
        [field, plain, field, field],
        u1xy,
        u1z,
        rc,
        rz,
        eps,
        fx,
        fv,
        name="apply_second",
    )
    rc, rz = swap(sz, sc)
    row, products = call(
        partial(products_kernel, strips),
        [(1, LANES), (2 * len(PRODUCTS) - 1, rows_x, rows_y)],
        row,
        b,
        u1xy,
        u1z,
        u2xy,
        u2z,
        name="products",
    )
    (rows,) = call(
        partial(third_kernel, strips),
        [(slabs, LANES)],
        row,
        b,
        u1xy,
        u1z,
        u2xy,
        u2z,
        rc,
        rz,
        eps,
        fx,
        fv,
        name="apply_third",
    )
    rows = lax.all_to_all(rows, "gz", 0, 0)
    (parts,) = call(
        partial(gradient_kernel, strips),
        [(shares, rows_x // shares, rows_y)],
        rows,
        products,
        fv,
        name="gradient",
    )
    parts = lax.all_to_all(parts, "wl", 0, 0)
    return jnp.sum(parts, axis=0)[None]


def solution(mesh):
    return jax.shard_map(
        body,
        mesh=mesh,
        in_specs=(
            P("wl", None, "gz", None, None),
            P("wl", None, "gz", None, None),
            P(None, "gz", None, None),
            P("wl"),
            P(),
            P("gz"),
        ),
        out_specs=P("gz", "wl", None),
        check_vma=False,
    )
```

time: 711 us -> 66.5 us (0.09)
  blocking collectives: 638 us -> 33 us
  waiting for transfers between devices: 24.8 us -> 11.9 us
  local copies, waits for them, and re-layouts: 13.1 us -> 0.65 us
  other arithmetic: 13.1 us -> 1.64 us
    psum x6 -> x0, blocking collectives: 638 us -> none  [the longest x2 254 us: body(): gram = lax.psum((gram_re, gram_im), 'gz')]
    all_to_all x0 -> x2, blocking collectives: none -> 33 us  [the longest x1 24.7 us: body(): rows = lax.all_to_all(rows, 'gz', 0, 0)]
    ppermute x6, waiting for transfers between devices: 24.8 us -> 11.9 us  [the longest x3 11.9 us: swap(): from_chip = lax.ppermute(to_chip, 'gz', chip_pairs)]
    unnamed x91 -> x4, local copies, waits for them, and re-layouts: 10.1 us -> 0.65 us
    sub x59 -> x0, other arithmetic: 8.04 us -> none  [the longest x5 2.52 us: scale_by(): coef_re * fields_re - coef_im * fields_im]
  transfers between devices with their start and end apart: 6 -> 6, of which waited for: 6 -> 3; matrix products, arithmetic and copies ran while one was open for 0% -> 0% of each run, Pallas kernels for 0% -> 2%
where the time goes in v1:
time: 66.5 us; the launch traced here: 66.2 us
  blocking collectives  33 us (50%)
  starting transfers between devices  13 us (20%)
  waiting for transfers between devices  11.9 us (18%)
  Pallas kernels  4.56 us (7%)
  other arithmetic  1.64 us (2%)
  between operations  1.41 us (2%)
    all_to_all x1, blocking collectives, body(): rows = lax.all_to_all(rows, 'gz', 0, 0)  24.7 us
    ppermute x3, starting transfers between devices, swap(): from_chip = lax.ppermute(to_chip, 'gz', chip_pairs)  12.8 us
    ppermute x3, waiting for transfers between devices, swap(): from_chip = lax.ppermute(to_chip, 'gz', chip_pairs)  11.9 us
    all_to_all x1, blocking collectives, body(): parts = lax.all_to_all(parts, 'wl', 0, 0)  8.37 us
    pallas_call x7, Pallas kernels, call(): pl.pallas_call(kernel, out_shape=shapes, in_specs=specs, out_specs=outs_s...  4.56 us
  transfers between devices with their start and end apart: 6, of which 3 were waited for; matrix products, arithmetic and copies ran while one was open for 0% of the time, Pallas kernels for 2%

profile of v1, /device:TPU:1, one launch (start us, length us, event | category | flops | bytes accessed | tf_op | source)
XLA Modules:
  0.0 66.2 jit_solution(7326011775914959824)
XLA Ops:
  0.0 1.0 %maximum_bitcast_fusion.refs_0_.refs_1_ = f32[2,3,96,128]{3,2,1,0:T(8,128)S(1)} fusion(f32[1,3,1,96,128]{4,3,1,0,2:T(8,128)} %bitcast.16, f32[1,3,1,96,128]{4,3,1,0,2:T(8,128)} %bitcast.17), kind=kLoop, calls=%fused_computation | loop fusion | flops 73728 | bytes 589824 | tf_op jit(solution)/shard_map/reshape | solution.py:468
  1.0 4.9 %collective-permute-start.1 = (f32[2,3,96,128]{3,2,1,0:T(8,128)S(1)}, f32[2,3,96,128]{3,2,1,0:T(8,128)S(1)}, u32[]{:S(2)}, u32[]{:S(2)}) collective-permute-start(f32[2,3,96,128]{3,2,1,0:T(8,128)S(1)} %maximum_bitcast_fusion.refs_0_.refs_1_), channel_id=1, source_target_pairs={{1,2},{2,1},{3,4},{4,3},{5,6},{6,5},{7,8},{8,7},{9,10},{10,9},{11,... | collective-permute-start | bytes 884744 | tf_op jit(solution)/shard_map/ppermute | solution.py:474
  6.0 0.1 collective-permute-start
  7.4 0.0 copy-start.1
  7.4 0.6 copy-done.1
  8.0 0.6 factors.1
  8.7 1.7 %collective-permute-done.1.refs_2_ = f32[2,3,96,128]{3,2,1,0:T(8,128)S(1)} collective-permute-done((f32[2,3,96,128]{3,2,1,0:T(8,128)S(1)}, f32[2,3,96,128]{3,2,1,0:T(8,128)S(1)}, u32[]{:S(2)}, u32[]{:S(2)}) %collective-permute-start.1) | collective-permute-done | bytes 294944 | tf_op jit(solution)/shard_map/ppermute | solution.py:474
  10.4 0.0 collective-permute-done.refs_1_
  10.4 0.9 %apply_first.1 = (f32[2,2,2,96,128]{4,3,2,1,0:T(8,128)S(1)}, f32[2,2,96,128]{3,2,1,0:T(8,128)S(1)}, f32[2,2,2,96,128]{4,3,2,1,0:T(8,128)S(1)}, f32[2,2,2,96,128]{4,3,2,1,0:T(8,128)S(1)}) custom-call(f32[2,3,96,128]{3,2,1,0:T(8,128)S(1)} %maximum_bitcast_fusion.refs_0_.refs_1_, f32[2,3,96,128]{3,2,1,0:T(8,128)S(1)} %collective-permute-done.refs_1_, ...), custom_call_target="tpu_custom_call" | custom-call | bytes 1282048 | tf_op jit(solution)/shard_map/apply_first/pallas_call | solution.py:440
  11.3 0.1 collective-permute-start.2
  11.4 3.9 %collective-permute-start.3 = (f32[2,2,2,96,128]{4,3,2,1,0:T(8,128)S(1)}, f32[2,2,2,96,128]{4,3,2,1,0:T(8,128)S(1)}, u32[]{:S(2)}, u32[]{:S(2)}) collective-permute-start(f32[2,2,2,96,128]{4,3,2,1,0:T(8,128)S(1)} %get-tuple-element.22), channel_id=1, source_target_pairs={{1,2},{2,1},{3,4},{4,3},{5,6},{6,5},{7,8},{8,7},{9,10},{10,9},{11,... | collective-permute-start | bytes 1179656 | tf_op jit(solution)/shard_map/ppermute | solution.py:474
  15.3 0.0 collective-permute-done.2.refs_2_
  15.3 5.4 %collective-permute-done.3.refs_3_ = f32[2,2,2,96,128]{4,3,2,1,0:T(8,128)S(1)} collective-permute-done((f32[2,2,2,96,128]{4,3,2,1,0:T(8,128)S(1)}, f32[2,2,2,96,128]{4,3,2,1,0:T(8,128)S(1)}, u32[]{:S(2)}, u32[]{:S(2)}) %collective-permute-start.3) | collective-permute-done | bytes 393248 | tf_op jit(solution)/shard_map/ppermute | solution.py:474
  20.7 1.0 %apply_second.1 = (f32[2,2,2,96,128]{4,3,2,1,0:T(8,128)S(1)}, f32[2,2,96,128]{3,2,1,0:T(8,128)S(1)}, f32[2,2,2,96,128]{4,3,2,1,0:T(8,128)S(1)}, f32[2,2,2,96,128]{4,3,2,1,0:T(8,128)S(1)}) custom-call(f32[2,2,2,96,128]{4,3,2,1,0:T(8,128)S(1)} %get-tuple-element.19.refs_1_.refs_0_.refs_2_, f32[2,2,96,128]{3,2,1,0:T(8,128)S(1)} %get-tuple-element.20.refs_2_.refs_1_.refs_3_, ...), custom_call_target="tpu_custom_call" | custom-call | bytes 1773568 | tf_op jit(solution)/shard_map/apply_second/pallas_call | solution.py:440
  21.8 0.1 collective-permute-start.4
  21.9 3.9 %collective-permute-start.5 = (f32[2,2,2,96,128]{4,3,2,1,0:T(8,128)S(1)}, f32[2,2,2,96,128]{4,3,2,1,0:T(8,128)S(1)}, u32[]{:S(2)}, u32[]{:S(2)}) collective-permute-start(f32[2,2,2,96,128]{4,3,2,1,0:T(8,128)S(1)} %get-tuple-element.27), channel_id=1, source_target_pairs={{1,2},{2,1},{3,4},{4,3},{5,6},{6,5},{7,8},{8,7},{9,10},{10,9},{11,... | collective-permute-start | bytes 1179656 | tf_op jit(solution)/shard_map/ppermute | solution.py:474
  25.8 0.2 sums.1.refs_0_
  26.0 0.5 products.1
  26.5 4.7 %collective-permute-done.5.refs_7_ = f32[2,2,2,96,128]{4,3,2,1,0:T(8,128)S(1)} collective-permute-done((f32[2,2,2,96,128]{4,3,2,1,0:T(8,128)S(1)}, f32[2,2,2,96,128]{4,3,2,1,0:T(8,128)S(1)}, u32[]{:S(2)}, u32[]{:S(2)}) %collective-permute-start.5) | collective-permute-done | bytes 393248 | tf_op jit(solution)/shard_map/ppermute | solution.py:474
  31.2 1.1 %apply_third.1 = f32[64,128]{1,0:T(8,128)S(1)} custom-call(f32[1,128]{1,0:T(1,128)S(1)} %get-tuple-element.25.refs_0_, f32[2,3,96,128]{3,2,1,0:T(8,128)S(1)} %maximum_bitcast_fusion.refs_0_.refs_1_, f32[2,2,2,96,128]{4,3,2,1,0:T(8,128)S(1)} %get-tuple-element.19.refs_1_.refs_0_.refs_2_, f32[2,2,96,128]{3,2,1,0:T(8,128)S(1)} %get-tuple-element.20.refs_2_.refs_1_.refs_3_, ...), custom_call_target="tpu_custom_call" | custom-call | bytes 2658816 | tf_op jit(solution)/shard_map/apply_third/pallas_call | solution.py:440
  32.3 24.7 %all_to_all.16 = f32[64,1,128]{2,1,0:T(1,128)S(1)} all-to-all(f32[64,1,128]{2,1,0:T(1,128)S(1)} %bitcast.14), channel_id=1, replica_groups=mesh['wl'=4,'gz'=64] {'gz'}, dimensions={0} | all-to-all | bytes 65536 | tf_op jit(solution)/shard_map/all_to_all | solution.py:542
  57.0 0.3 gradient.1
  57.2 8.4 %all_to_all.17 = f32[4,24,128]{2,1,0:T(8,128)S(1)} all-to-all(f32[4,24,128]{2,1,0:T(8,128)S(1)} %gradient.1), channel_id=1, replica_groups=mesh['wl'=4,'gz'=64] {'wl'}, dimensions={0} | all-to-all | bytes 98304 | tf_op jit(solution)/shard_map/all_to_all | solution.py:551
  65.6 0.6 reduce_sum.9
  (3 shorter events, 0.0 us)
Async XLA Ops:
  0.0 10.4 %copy-start = (f32[3,1,96,128]{3,2,1,0:T(8,128)S(1)}, f32[3,1,96,128]{3,2,1,0:T(8,128)}, u32[]{:S(2)}) copy-start(f32[3,1,96,128]{3,2,1,0:T(8,128)} %param.8) | copy-start | bytes 442372
  1.0 9.3 %collective-permute-start.1 = (f32[2,3,96,128]{3,2,1,0:T(8,128)S(1)}, f32[2,3,96,128]{3,2,1,0:T(8,128)S(1)}, u32[]{:S(2)}, u32[]{:S(2)}) collective-permute-start(f32[2,3,96,128]{3,2,1,0:T(8,128)S(1)} %maximum_bitcast_fusion.refs_0_.refs_1_), channel_id=1, source_target_pairs={{1,2},{2,1},{3,4},{4,3},{5,6},{6,5},{7,8},{8,7},{9,10},{10,9},{11,... | collective-permute-start | bytes 884744 | tf_op jit(solution)/shard_map/ppermute | solution.py:474
  6.0 4.4 %collective-permute-start = (f32[2,3,96,128]{3,2,1,0:T(8,128)S(1)}, f32[2,3,96,128]{3,2,1,0:T(8,128)S(1)}, u32[]{:S(2)}, u32[]{:S(2)}) collective-permute-start(f32[2,3,96,128]{3,2,1,0:T(8,128)S(1)} %maximum_bitcast_fusion.refs_0_.refs_1_), channel_id=1, source_target_pairs={{0,1},{1,0},{2,3},{3,2},{4,5},{5,4},{6,7},{7,6},{8,9},{9,8},{10,11... | collective-permute-start | bytes 884744 | tf_op jit(solution)/shard_map/ppermute | solution.py:475
  7.4 0.7 copy-start.1
  11.3 4.0 %collective-permute-start.2 = (f32[2,2,2,96,128]{4,3,2,1,0:T(8,128)S(1)}, f32[2,2,2,96,128]{4,3,2,1,0:T(8,128)S(1)}, u32[]{:S(2)}, u32[]{:S(2)}) collective-permute-start(f32[2,2,2,96,128]{4,3,2,1,0:T(8,128)S(1)} %get-tuple-element.21), channel_id=1, source_target_pairs={{0,1},{1,0},{2,3},{3,2},{4,5},{5,4},{6,7},{7,6},{8,9},{9,8},{10,11... | collective-permute-start | bytes 1179656 | tf_op jit(solution)/shard_map/ppermute | solution.py:475
  11.4 9.4 %collective-permute-start.3 = (f32[2,2,2,96,128]{4,3,2,1,0:T(8,128)S(1)}, f32[2,2,2,96,128]{4,3,2,1,0:T(8,128)S(1)}, u32[]{:S(2)}, u32[]{:S(2)}) collective-permute-start(f32[2,2,2,96,128]{4,3,2,1,0:T(8,128)S(1)} %get-tuple-element.22), channel_id=1, source_target_pairs={{1,2},{2,1},{3,4},{4,3},{5,6},{6,5},{7,8},{8,7},{9,10},{10,9},{11,... | collective-permute-start | bytes 1179656 | tf_op jit(solution)/shard_map/ppermute | solution.py:474
  21.8 4.8 %collective-permute-start.4 = (f32[2,2,2,96,128]{4,3,2,1,0:T(8,128)S(1)}, f32[2,2,2,96,128]{4,3,2,1,0:T(8,128)S(1)}, u32[]{:S(2)}, u32[]{:S(2)}) collective-permute-start(f32[2,2,2,96,128]{4,3,2,1,0:T(8,128)S(1)} %get-tuple-element.26), channel_id=1, source_target_pairs={{0,1},{1,0},{2,3},{3,2},{4,5},{5,4},{6,7},{7,6},{8,9},{9,8},{10,11... | collective-permute-start | bytes 1179656 | tf_op jit(solution)/shard_map/ppermute | solution.py:475
  21.9 9.4 %collective-permute-start.5 = (f32[2,2,2,96,128]{4,3,2,1,0:T(8,128)S(1)}, f32[2,2,2,96,128]{4,3,2,1,0:T(8,128)S(1)}, u32[]{:S(2)}, u32[]{:S(2)}) collective-permute-start(f32[2,2,2,96,128]{4,3,2,1,0:T(8,128)S(1)} %get-tuple-element.27), channel_id=1, source_target_pairs={{1,2},{2,1},{3,4},{4,3},{5,6},{6,5},{7,8},{8,7},{9,10},{10,9},{11,... | collective-permute-start | bytes 1179656 | tf_op jit(solution)/shard_map/ppermute | solution.py:474

commit v2 on v1

--- a/solution.py
+++ b/solution.py
@@ -84,27 +84,38 @@
     pos = laneids().astype(jnp.float32)
     fv[0], fv[1] = profile(pos + 0.5, LANES, wy, angular)
     fv[2], fv[3] = profile(pos, LANES, wy, angular)
-    plane = jnp.broadcast_to(slab.astype(jnp.float32), (ROWS, LANES))
-    fv[4], fv[5] = profile(plane + 0.5, total_planes, wz, angular)
-    fv[6], fv[7] = profile(plane, total_planes, wz, angular)
-    below_re, below_im = profile(plane - 0.5, total_planes, wz, angular)
-    inside = plane > 0.0
-    fv[8] = jnp.where(inside, below_re, 0.0)
-    fv[9] = jnp.where(inside, below_im, 0.0)
-    fv[10] = jnp.broadcast_to(angular * angular, (ROWS, LANES))
-    fv[11] = jnp.broadcast_to((slab % 2).astype(jnp.float32), (ROWS, LANES))
-    fv[12] = jnp.broadcast_to(mask[0].astype(jnp.float32), (ROWS, LANES))
+    fv[4] = jnp.broadcast_to(angular * angular, (ROWS, LANES))
+    fv[5] = jnp.broadcast_to((slab % 2).astype(jnp.float32), (ROWS, LANES))
+    fv[6] = jnp.broadcast_to(mask[0].astype(jnp.float32), (ROWS, LANES))
+    side = 1 - 2 * (slab % 2)
+    for n, at_plane in enumerate((slab, slab - side, slab - 2 * side, slab + side)):
+        plane = jnp.broadcast_to(at_plane.astype(jnp.float32), (ROWS, LANES))
+        low = 7 + 7 * n
+        fv[low], fv[low + 1] = profile(plane + 0.5, total_planes, wz, angular)
+        fv[low + 2], fv[low + 3] = profile(plane, total_planes, wz, angular)
+        below_re, below_im = profile(plane - 0.5, total_planes, wz, angular)
+        above_floor = plane > 0.0
+        fv[low + 4] = jnp.where(above_floor, below_re, 0.0)
+        fv[low + 5] = jnp.where(above_floor, below_im, 0.0)
+        inside = (plane >= 0.0) & (plane < total_planes)
+        fv[low + 6] = jnp.where(inside, 1.0, 0.0)
+
+
+OWN, CHIP, BEHIND, CORE = 0, 1, 2, 3
+FACTOR_BLOCKS = 35
 
 
 class Factors:
-    def __init__(self, fv, fx):
+    def __init__(self, fv, fx, which=OWN):
+        low = 7 + 7 * which
         self.yh = (fv[0], fv[1])
         self.ye = (fv[2], fv[3])
-        self.zh = (fv[4], fv[5])
-        self.ze = (fv[6], fv[7])
-        self.zb = (fv[8], fv[9])
-        self.weight = fv[10]
-        self.upper_core = fv[11] > 0.5
+        self.weight = fv[4]
+        self.upper_core = fv[5] > 0.5
+        self.zh = (fv[low], fv[low + 1])
+        self.ze = (fv[low + 2], fv[low + 3])
+        self.zb = (fv[low + 4], fv[low + 5])
+        self.inside = fv[low + 6]
         self.fx = fx
 
     def x(self, s):
@@ -112,15 +123,21 @@
         return (self.fx[0, at, :], self.fx[1, at, :]), (self.fx[2, at, :], self.fx[3, at, :])
 
 
-ZERO = 0.0
-
-
 def zeros():
     return jnp.zeros((ROWS, LANES), jnp.float32)
 
 
+def no_strip():
+    nil = (zeros(), zeros())
+    return nil, nil
+
+
 def rmul(factor, real):
     return factor[0] * real, factor[1] * real
+
+
+def here(s):
+    return pl.ds(s * ROWS, ROWS)
 
 
 def curl_of(fac, sh, xe, hx, hy, hz, hx_b, hy_b, before):
@@ -133,83 +150,83 @@
     return cx, cy, cz
 
 
-def first_apply(fac, sh, b, rc, rz, eps, q, s, strips, before):
-    at = pl.ds(s * ROWS, ROWS)
-    after = pl.ds((s + 1) * ROWS, ROWS)
-    last = s + 1 == strips
-    core = fac.upper_core
-
-    def up(c):
-        return jnp.where(core, rz[q, c, at, :], rc[q, c, at, :])
-
-    def dn(c, where):
-        return jnp.where(core, rc[q, c, where, :], rz[q, c, where, :])
-
-    ex, ey, ez = (b[q, c, at, :] for c in range(3))
-    nxt = lambda c: zeros() if last else b[q, c, after, :]
+def real_apply(fac, sh, lo, mid, hi, eps, s, strips, before):
+    at = here(s)
+    after = lambda of, c: zeros() if s + 1 == strips else of(c, here(s + 1))
+    ex, ey, ez = (mid(c, at) for c in range(3))
     xh, xe = fac.x(s)
-    dx_ez = sh.x_next(ez, nxt(2)) - ez
-    dx_ey = sh.x_next(ey, nxt(1)) - ey
+    dx_ez = sh.x_next(ez, after(mid, 2)) - ez
+    dx_ey = sh.x_next(ey, after(mid, 1)) - ey
     dy_ez = sh.y_next(ez) - ez
     dy_ex = sh.y_next(ex) - ex
-    hx = csub(rmul(fac.yh, dy_ez), rmul(fac.zh, up(1) - ey))
-    hy = csub(rmul(fac.zh, up(0) - ex), rmul(xh, dx_ez))
+    hx = csub(rmul(fac.yh, dy_ez), rmul(fac.zh, hi(1, at) - ey))
+    hy = csub(rmul(fac.zh, hi(0, at) - ex), rmul(xh, dx_ez))
     hz = csub(rmul(xh, dx_ey), rmul(fac.yh, dy_ex))
-    bx, by, bz = (dn(c, at) for c in range(3))
-    dx_bz = sh.x_next(bz, zeros() if last else dn(2, after)) - bz
+    bx, by, bz = (lo(c, at) for c in range(3))
+    dx_bz = sh.x_next(bz, after(lo, 2)) - bz
     dy_bz = sh.y_next(bz) - bz
     hx_b = csub(rmul(fac.yh, dy_bz), rmul(fac.zb, ey - by))
     hy_b = csub(rmul(fac.zb, ex - bx), rmul(xh, dx_bz))
     curls = curl_of(fac, sh, xe, hx, hy, hz, hx_b, hy_b, before)
     out = []
     for c, e in enumerate((ex, ey, ez)):
-        out.append((curls[c][0] - fac.weight * eps[c, at, :] * e, curls[c][1]))
+        out.append((curls[c][0] - fac.weight * eps(c, at) * e, curls[c][1]))
     return out, (hy, hz)
 
 
-def next_apply(fac, sh, exy, ez_ref, rc, rz, eps, q, s, strips, before, shift):
-    at = pl.ds(s * ROWS, ROWS)
-    after = pl.ds((s + 1) * ROWS, ROWS)
-    last = s + 1 == strips
-    core = fac.upper_core
-    up = lambda c: tuple(jnp.where(core, rz[c, q, p, at, :], rc[c, q, p, at, :]) for p in range(2))
-    dn = lambda c: tuple(jnp.where(core, rc[c, q, p, at, :], rz[c, q, p, at, :]) for p in range(2))
-    ex = tuple(exy[0, q, p, at, :] for p in range(2))
-    ey = tuple(exy[1, q, p, at, :] for p in range(2))
-    ez = tuple(ez_ref[q, p, at, :] for p in range(2))
-    ey_n = tuple(zeros() if last else exy[1, q, p, after, :] for p in range(2))
-    ez_n = tuple(zeros() if last else ez_ref[q, p, after, :] for p in range(2))
+def complex_apply(fac, sh, mid, up, below, eps, s, strips, before, shift):
+    at = here(s)
+    nil = (zeros(), zeros())
+    after = lambda c: nil if s + 1 == strips else mid(c, here(s + 1))
+    ex, ey, ez = (mid(c, at) for c in range(3))
     xh, xe = fac.x(s)
     dfx = lambda v, n: tuple(sh.x_next(a, b) - a for a, b in zip(v, n))
     dfy = lambda v: tuple(sh.y_next(a) - a for a in v)
-    hx = csub(cmul(fac.yh, dfy(ez)), cmul(fac.zh, csub(up(1), ey)))
-    hy = csub(cmul(fac.zh, csub(up(0), ex)), cmul(xh, dfx(ez, ez_n)))
-    hz = csub(cmul(xh, dfx(ey, ey_n)), cmul(fac.yh, dfy(ex)))
-    hx_b = csub(dn(0), cmul(fac.zb, ey))
-    hy_b = cadd(dn(1), cmul(fac.zb, ex))
+    hx = csub(cmul(fac.yh, dfy(ez)), cmul(fac.zh, csub(up(1, at), ey)))
+    hy = csub(cmul(fac.zh, csub(up(0, at), ex)), cmul(xh, dfx(ez, after(2))))
+    hz = csub(cmul(xh, dfx(ey, after(1))), cmul(fac.yh, dfy(ex)))
+    hx_b, hy_b = below(ex, ey)
     curls = curl_of(fac, sh, xe, hx, hy, hz, hx_b, hy_b, before)
     out = []
     for c, e in enumerate((ex, ey, ez)):
-        diagonal = fac.weight * eps[c, at, :] + shift
+        diagonal = fac.weight * eps(c, at) + shift
         out.append(tuple(curls[c][p] - diagonal * e[p] for p in range(2)))
     return out, (hy, hz)
 
 
-def store_field(fac, sh, field, q, s, strips, held, uxy, uz, sc, sz):
-    at = pl.ds(s * ROWS, ROWS)
-    for c in range(2):
-        for p in range(2):
-            uxy[c, q, p, at, :] = field[c][p]
-    for p in range(2):
-        uz[q, p, at, :] = field[2][p]
-    if held is not None:
-        store_sends(fac, sh, held, field[2], q, s - 1, sc, sz)
-    if s + 1 == strips:
-        store_sends(fac, sh, field, (zeros(), zeros()), q, s, sc, sz)
+def plane_of(ref, q):
+    return lambda c, at: ref[3 * q + c, at, :]
+
+
+def eps_of(ref):
+    return lambda c, at: ref[6 + c, at, :]
+
+
+def either(mask, yes, no):
+    return lambda c, at: jnp.where(mask, yes(c, at), no(c, at))
+
+
+def field_of(uxy, uz, q):
+    def read(c, at):
+        ref = uz.at[q] if c == 2 else uxy.at[c, q]
+        return ref[0, at, :], ref[1, at, :]
+
+    return read
+
+
+def side_of(ref, q):
+    return lambda c, at: (ref[c, q, 0, at, :], ref[c, q, 1, at, :])
+
+
+def either_pair(mask, yes, no):
+    def read(c, at):
+        return tuple(jnp.where(mask, a, b) for a, b in zip(yes(c, at), no(c, at)))
+
+    return read
 
 
 def store_sends(fac, sh, field, ez_n, q, s, sc, sz):
-    at = pl.ds(s * ROWS, ROWS)
+    at = here(s)
     xh, _ = fac.x(s)
     ex, ey, ez = field
     dx_ez = tuple(sh.x_next(a, b) - a for a, b in zip(ez, ez_n))
@@ -219,32 +236,161 @@
     part_y = (-part_y[0], -part_y[1])
     for c, (down, above) in enumerate(((ex, part_x), (ey, part_y))):
         for p in range(2):
-            sc[c, q, p, at, :] = jnp.where(fac.upper_core, down[p], above[p])
-            sz[c, q, p, at, :] = jnp.where(fac.upper_core, above[p], down[p])
-
-
-def first_kernel(strips, b, rc, rz, eps, fx, fv, uxy, uz, sc, sz):
+            if sc is not None:
+                sc[c, q, p, at, :] = jnp.where(fac.upper_core, down[p], above[p])
+            if sz is not None:
+                sz[c, q, p, at, :] = jnp.where(fac.upper_core, above[p], down[p])
+
+
+def store_field(field, q, s, uxy, uz):
+    for p in range(2):
+        for c in range(2):
+            uxy[c, q, p, here(s), :] = field[c][p]
+        uz[q, p, here(s), :] = field[2][p]
+
+
+def with_sends(fac, sh, q, strips, sc, sz, strips_of):
+    held = []
+
+    def store(field, s):
+        if held:
+            store_sends(fac, sh, held.pop(), field[2], q, s - 1, sc, sz)
+        held.append(field)
+
+    strips_of(store)
+    store_sends(fac, sh, held.pop(), (zeros(), zeros()), q, strips - 1, sc, sz)
+
+
+def real_strips(fac, sh, lo, mid, hi, eps, strips, store):
+    before = no_strip()
+    for s in range(strips):
+        field, before = real_apply(fac, sh, lo, mid, hi, eps, s, strips, before)
+        store(field, s)
+
+
+def complex_strips(fac, sh, eps, uxy, uz, rc, rz, q, strips, shift, store):
+    core = fac.upper_core
+    before = no_strip()
+    up = either_pair(core, side_of(rz, q), side_of(rc, q))
+    dn = either_pair(core, side_of(rc, q), side_of(rz, q))
+    for s in range(strips):
+
+        def below(ex, ey):
+            at = here(s)
+            return csub(dn(0, at), cmul(fac.zb, ey)), cadd(dn(1, at), cmul(fac.zb, ex))
+
+        field, before = complex_apply(
+            fac, sh, field_of(uxy, uz, q), up, below, eps, s, strips, before, shift
+        )
+        store(field, s)
+
+
+def masked(fac, field):
+    return [tuple(v * fac.inside for v in pair) for pair in field]
+
+
+def own_kernel(strips, x, ca, za, fx, fv, uxy, uz, sz):
+    fac, sh = Factors(fv, fx), Shifts()
+    core = fac.upper_core
+    for q in range(2):
+        hi = either(core, plane_of(za, q), plane_of(ca, q))
+        lo = either(core, plane_of(ca, q), plane_of(za, q))
+
+        def run(store):
+            def both(field, s):
+                store_field(field, q, s, uxy, uz)
+                store(field, s)
+
+            real_strips(fac, sh, lo, plane_of(x, q), hi, eps_of(x), strips, both)
+
+        with_sends(fac, sh, q, strips, None, sz, run)
+
+
+def side_kernel(strips, x, za, zb, fx, fv, uxy, uz, rz):
+    fac, sh = Factors(fv, fx, CHIP), Shifts()
+    core = fac.upper_core
+    for q in range(2):
+        hi = either(core, plane_of(zb, q), plane_of(x, q))
+        lo = either(core, plane_of(x, q), plane_of(zb, q))
+
+        def run(store):
+            def both(field, s):
+                field = masked(fac, field)
+                store_field(field, q, s, uxy, uz)
+                store(field, s)
+
+            real_strips(fac, sh, lo, plane_of(za, q), hi, eps_of(za), strips, both)
+
+        with_sends(fac, sh, q, strips, rz, None, run)
+
+
+def core_kernel(strips, x, ca, cb, fx, fv, rc):
+    fac, sh = Factors(fv, fx, CORE), Shifts()
+    core = fac.upper_core
+    for q in range(2):
+        hi = either(core, plane_of(x, q), plane_of(cb, q))
+        lo = either(core, plane_of(cb, q), plane_of(x, q))
+
+        def run(store):
+            real_strips(fac, sh, lo, plane_of(ca, q), hi, eps_of(ca), strips, store)
+
+        with_sends(fac, sh, q, strips, None, rc, run)
+
+
+def second_kernel(strips, x, u1xy, u1z, rc, rz, fx, fv, uxy, uz, sc):
     fac, sh = Factors(fv, fx), Shifts()
     for q in range(2):
-        nil = (zeros(), zeros())
-        before, held = (nil, nil), None
-        for s in range(strips):
-            field, before = first_apply(fac, sh, b, rc, rz, eps, q, s, strips, before)
-            store_field(fac, sh, field, q, s, strips, held, uxy, uz, sc, sz)
-            held = field
-
-
-def second_kernel(strips, exy, ez, rc, rz, eps, fx, fv, uxy, uz, sc, sz):
+
+        def run(store):
+            def both(field, s):
+                store_field(field, q, s, uxy, uz)
+                store(field, s)
+
+            complex_strips(
+                fac, sh, eps_of(x), u1xy, u1z, rc, rz, q, strips, SHIFT[1], both
+            )
+
+        with_sends(fac, sh, q, strips, sc, None, run)
+
+
+def behind_kernel(strips, za, zb, zc, sz, side_xy, side_z, fx, fv, rz2, rz1):
+    sh = Shifts()
+    for q in range(2):
+        fac = Factors(fv, fx, BEHIND)
+        core = fac.upper_core
+        hi = either(core, plane_of(zc, q), plane_of(za, q))
+        lo = either(core, plane_of(za, q), plane_of(zc, q))
+
+        def run_first(store):
+            masked_store = lambda field, s: store(masked(fac, field), s)
+            real_strips(fac, sh, lo, plane_of(zb, q), hi, eps_of(zb), strips, masked_store)
+
+        with_sends(fac, sh, q, strips, rz1, None, run_first)
+    for q in range(2):
+        fac = Factors(fv, fx, CHIP)
+
+        def run_second(store):
+            masked_store = lambda field, s: store(masked(fac, field), s)
+            complex_strips(
+                fac, sh, eps_of(za), side_xy, side_z, sz, rz1, q, strips, SHIFT[1], masked_store
+            )
+
+        with_sends(fac, sh, q, strips, rz2, None, run_second)
+
+
+def third_kernel(strips, before, x, u1xy, u1z, u2xy, u2z, rc, rz, fx, fv, row):
     fac, sh = Factors(fv, fx), Shifts()
+    sums = {}
     for q in range(2):
-        nil = (zeros(), zeros())
-        before, held = (nil, nil), None
-        for s in range(strips):
-            field, before = next_apply(
-                fac, sh, exy, ez, rc, rz, eps, q, s, strips, before, SHIFT[1]
-            )
-            store_field(fac, sh, field, q, s, strips, held, uxy, uz, sc, sz)
-            held = field
+
+        def store(u3, s):
+            u = [source_of(x, q, s), strip_of(u1xy, u1z, q, s), strip_of(u2xy, u2z, q, s), u3]
+            for g, (i, j) in enumerate(GRAM):
+                if j == 3:
+                    add_sums(sums, g, q, dot_strip(u[i], u[j]))
+
+        complex_strips(fac, sh, eps_of(x), u2xy, u2z, rc, rz, q, strips, SHIFT[2], store)
+    row[...] = jnp.broadcast_to(before[...] + gather_sums(sums), row.shape)
 
 
 def strip_of(uxy, uz, q, s):
@@ -254,9 +400,8 @@
     ]
 
 
-def source_of(b, q, s):
-    at = pl.ds(s * ROWS, ROWS)
-    return [(b[q, c, at, :],) for c in range(3)]
+def source_of(x, q, s):
+    return [(x[3 * q + c, here(s), :],) for c in range(3)]
 
 
 def times(a, b):
@@ -321,23 +466,6 @@
                 products[place, at, :] = part
                 place += 1
     row[...] = before[...] + gather_sums(sums)
-
-
-def third_kernel(strips, before, b, u1xy, u1z, u2xy, u2z, rc, rz, eps, fx, fv, row):
-    fac, sh = Factors(fv, fx), Shifts()
-    sums = {}
-    for q in range(2):
-        nil = (zeros(), zeros())
-        prior = (nil, nil)
-        for s in range(strips):
-            u3, prior = next_apply(
-                fac, sh, u2xy, u2z, rc, rz, eps, q, s, strips, prior, SHIFT[2]
-            )
-            u = [source_of(b, q, s), strip_of(u1xy, u1z, q, s), strip_of(u2xy, u2z, q, s), u3]
-            for g, (i, j) in enumerate(GRAM):
-                if j == 3:
-                    add_sums(sums, g, q, dot_strip(u[i], u[j]))
-    row[...] = jnp.broadcast_to(before[...] + gather_sums(sums), row.shape)
 
 
 def coefficients(gram):
@@ -412,7 +540,7 @@
             parts.append(jnp.broadcast_to(picked, (ROWS, LANES)))
         gram[pair] = tuple(parts)
     coefs = coefficients(gram)
-    scale = fv[10] * fv[12]
+    scale = fv[4] * fv[6]
     one_row = lambda v, q: jnp.broadcast_to(v[q : q + 1, :], (ROWS, LANES))
     weights = []
     for i, j in PRODUCTS:
@@ -432,18 +560,18 @@
         out[s // per_share, pl.ds((s % per_share) * ROWS, ROWS), :] = value
 
 
-def call(kernel, outs, *args, smem=0, name=None, flops=0):
+def call(kernel, outs, *args, smem=0, name=None, flops=0, cost=1, scratch=()):
     specs = [pl.BlockSpec(memory_space=pltpu.SMEM if i < smem else VM) for i in range(len(args))]
     shapes = [jax.ShapeDtypeStruct(s, jnp.float32) for s in outs]
     outs_spec = [pl.BlockSpec(memory_space=VM) for _ in outs]
-    nbytes = sum(4 * a.size for a in args)
     return pl.pallas_call(
         kernel,
         out_shape=shapes,
         in_specs=specs,
         out_specs=outs_spec,
+        scratch_shapes=[VM(s, jnp.float32) for s in scratch],
         name=name,
-        cost_estimate=pl.CostEstimate(flops=flops, bytes_accessed=nbytes, transcendentals=0),
+        cost_estimate=pl.CostEstimate(flops=flops, bytes_accessed=cost, transcendentals=0),
         compiler_params=pltpu.CompilerParams(vmem_limit_bytes=32 * 1024 * 1024),
     )(*args)
 
@@ -464,21 +592,30 @@
     chip_pairs = []
     for i in range(1, slabs - 1, 2):
         chip_pairs += [(i, i + 1), (i + 1, i)]
+    behind_pairs = [(i, i + 2) for i in range(0, slabs - 2, 2)]
+    behind_pairs += [(i, i - 2) for i in range(3, slabs, 2)]
     place = lax.axis_index("gz").astype(jnp.int32).reshape(1)
-    b = jnp.concatenate([source_fwd, source_adj], axis=0).reshape(2, 3, rows_x, rows_y)
-    eps = permittivity.reshape(3, rows_x, rows_y)
+    x = jnp.concatenate(
+        [a.reshape(3, rows_x, rows_y) for a in (source_fwd, source_adj, permittivity)], axis=0
+    )
     field = (2, 2, 2, rows_x, rows_y)
     plain = (2, 2, rows_x, rows_y)
 
-    def swap(to_chip, to_core):
-        from_chip = lax.ppermute(to_chip, "gz", chip_pairs)
-        from_core = lax.ppermute(to_core, "gz", core_pairs)
-        return from_core, from_chip
-
-    rc, rz = swap(b, b)
+    def behind(value):
+        return lax.ppermute(value, "gz", behind_pairs)
+
+    def core_swap(value):
+        return lax.ppermute(value, "gz", core_pairs)
+
+    za = lax.ppermute(x, "gz", chip_pairs)
+    zb = behind(x)
+    ca = core_swap(x)
+    cb = core_swap(za[:6])
+    zc = behind(za[:6])
+    za, zb, ca, cb = lax.optimization_barrier((za, zb, ca, cb))
     fx, fv = call(
         partial(factor_kernel, slabs, rows_x),
-        [(4, rows_x, rows_y), (13, ROWS, LANES)],
+        [(4, rows_x, rows_y), (FACTOR_BLOCKS, ROWS, LANES)],
         pml_widths,
         omegas,
         design_mask,
@@ -486,55 +623,65 @@
         smem=4,
         name="factors",
     )
-    u1xy, u1z, sc, sz = call(
-        partial(first_kernel, strips),
-        [field, plain, field, field],
-        b,
-        rc,
-        rz,
-        eps,
-        fx,
-        fv,
-        name="apply_first",
-    )
-    rc, rz = swap(sz, sc)
-    (row,) = call(partial(sums_kernel, strips), [(1, LANES)], b, u1xy, u1z, name="sums")
-    u2xy, u2z, sc, sz = call(
+    u1xy, u1z, sz = call(
+        partial(own_kernel, strips), [field, plain, field], x, ca, za, fx, fv, name="apply_own"
+    )
+    (rc,) = call(partial(core_kernel, strips), [field], x, ca, cb, fx, fv, name="apply_core")
+    side_xy, side_z, rz = call(
+        partial(side_kernel, strips), [field, plain, field], x, za, zb, fx, fv, name="apply_side"
+    )
+    (row,) = call(partial(sums_kernel, strips), [(1, LANES)], x, u1xy, u1z, name="sums")
+    u2xy, u2z, sc = call(
         partial(second_kernel, strips),
-        [field, plain, field, field],
+        [field, plain, field],
+        x,
         u1xy,
         u1z,
         rc,
         rz,
-        eps,
         fx,
         fv,
         name="apply_second",
     )
-    rc, rz = swap(sz, sc)
+    rc = core_swap(sc)
     row, products = call(
         partial(products_kernel, strips),
         [(1, LANES), (2 * len(PRODUCTS) - 1, rows_x, rows_y)],
         row,
-        b,
+        x,
         u1xy,
         u1z,
         u2xy,
         u2z,
         name="products",
     )
+    (rz,) = call(
+        partial(behind_kernel, strips),
+        [field],
+        za,
+        zb,
+        zc,
+        sz,
+        side_xy,
+        side_z,
+        fx,
+        fv,
+        name="apply_behind",
+        scratch=[field],
+        flops=1 << 36,
+        cost=1 << 27,
+    )
     (rows,) = call(
         partial(third_kernel, strips),
         [(slabs, LANES)],
         row,
-        b,
+        x,
         u1xy,
         u1z,
         u2xy,
         u2z,
         rc,
         rz,
-        eps,
         fx,
         fv,
         name="apply_third",

time: 66.5 us -> 59.6 us (0.90)
  waiting for transfers between devices: 11.9 us -> 5.9 us
  Pallas kernels: 4.56 us -> 9.12 us
  blocking collectives: 33 us -> 29.4 us
  starting transfers between devices: 13 us -> 11.1 us
    ppermute x6, waiting for transfers between devices: 11.9 us -> 5.9 us  [the longest x1 5.88 us: body(): za = lax.ppermute(x, 'gz', chip_pairs)]
    pallas_call x7 -> x10, Pallas kernels: 4.56 us -> 9.12 us  [call(): pl.pallas_call(kernel, out_shape=shapes, in_specs=specs, out_specs=outs_s...]
    all_to_all x1, blocking collectives: 24.7 us -> 21 us  [body(): rows = lax.all_to_all(rows, 'gz', 0, 0)]
    ppermute x6, starting transfers between devices: 13 us -> 11.1 us  [the longest x1 4.94 us: body(): za = lax.ppermute(x, 'gz', chip_pairs)]
    concatenate x0 -> x1, other arithmetic: none -> 1.08 us  [body(): jnp.concatenate([a.reshape(3, rows_x, rows_y) for a in (source_fwd, sourc...]
    reshape x1 -> x0, other arithmetic: 1.04 us -> none  [body(): jnp.concatenate([source_fwd, source_adj], axis=0)]
  transfers between devices with their start and end apart: 6 -> 6, of which waited for: 3 -> 1; matrix products, arithmetic and copies ran while one was open for 0% -> 0% of each run, Pallas kernels for 2% -> 13%
where the time goes in v2:
time: 59.6 us; the launch traced here: 59.3 us
  blocking collectives  29.4 us (49%)
  starting transfers between devices  11.1 us (19%)
  Pallas kernels  9.12 us (15%)
  waiting for transfers between devices  5.9 us (10%)
  other arithmetic  1.69 us (3%)
  between operations  1.44 us (2%)
  local copies, waits for them, and re-layouts  0.67 us (1%)
    all_to_all x1, blocking collectives, body(): rows = lax.all_to_all(rows, 'gz', 0, 0)  21 us
    pallas_call x10, Pallas kernels, call(): pl.pallas_call(kernel, out_shape=shapes, in_specs=specs, out_specs=outs_s...  9.12 us
    all_to_all x1, blocking collectives, body(): parts = lax.all_to_all(parts, 'wl', 0, 0)  8.37 us
    ppermute x1, waiting for transfers between devices, body(): za = lax.ppermute(x, 'gz', chip_pairs)  5.88 us
    ppermute x1, starting transfers between devices, body(): za = lax.ppermute(x, 'gz', chip_pairs)  4.94 us
    ppermute x3, starting transfers between devices, core_swap(): return lax.ppermute(value, 'gz', core_pairs)  3.6 us
    ppermute x2, starting transfers between devices, behind(): return lax.ppermute(value, 'gz', behind_pairs)  2.58 us
  transfers between devices with their start and end apart: 6, of which 1 were waited for; matrix products, arithmetic and copies ran while one was open for 0% of the time, Pallas kernels for 13%

profile of v2, /device:TPU:1, one launch (start us, length us, event | category | flops | bytes accessed | tf_op | source)
XLA Modules:
  0.0 59.3 jit_solution(11122159805160604579)
XLA Ops:
  0.0 1.1 %pad_maximum_fusion.refs_0_.refs_1_ = f32[9,96,128]{2,1,0:T(8,128)S(1)} fusion(f32[3,96,128]{2,1,0:T(8,128)} %bitcast.11, f32[3,96,128]{2,1,0:T(8,128)} %bitcast.12, f32[3,96,128]{2,1,0:T(8,128)} %bitcast.13), kind=kLoop, calls=%fused_computation | loop fusion | flops 221184 | bytes 884736 | tf_op jit(solution)/shard_map/concatenate | solution.py:598
  1.1 4.9 %collective-permute-start = (f32[9,96,128]{2,1,0:T(8,128)S(1)}, f32[9,96,128]{2,1,0:T(8,128)S(1)}, u32[]{:S(2)}, u32[]{:S(2)}) collective-permute-start(f32[9,96,128]{2,1,0:T(8,128)S(1)} %pad_maximum_fusion.refs_0_.refs_1_), channel_id=1, source_target_pairs={{1,2},{2,1},{3,4},{4,3},{5,6},{6,5},{7,8},{8,7},{9,10},{10,9},{11,... | collective-permute-start | bytes 1327112 | tf_op jit(solution)/shard_map/ppermute | solution.py:610
  6.0 0.1 collective-permute-start.2
  6.1 1.3 %collective-permute-start.1 = (f32[9,96,128]{2,1,0:T(8,128)S(1)}, f32[9,96,128]{2,1,0:T(8,128)S(1)}, u32[]{:S(2)}, u32[]{:S(2)}) collective-permute-start(f32[9,96,128]{2,1,0:T(8,128)S(1)} %pad_maximum_fusion.refs_0_.refs_1_), channel_id=1, source_target_pairs={{0,2},{2,4},{4,6},{6,8},{8,10},{10,12},{12,14},{14,16},{16,18},{18... | collective-permute-start | bytes 1327112 | tf_op jit(solution)/shard_map/ppermute | solution.py:605
  7.4 5.9 %collective-permute-done.refs_2_.refs_1_.refs_0_ = f32[9,96,128]{2,1,0:T(8,128)S(1)} collective-permute-done((f32[9,96,128]{2,1,0:T(8,128)S(1)}, f32[9,96,128]{2,1,0:T(8,128)S(1)}, u32[]{:S(2)}, u32[]{:S(2)}) %collective-permute-start) | collective-permute-done | bytes 442400 | tf_op jit(solution)/shard_map/ppermute | solution.py:610
  13.3 0.1 collective-permute-start.3
  13.4 1.3 %collective-permute-start.5 = (f32[6,96,128]{2,1,0:T(8,128)S(1)}, f32[6,96,128]{2,1,0:T(8,128)S(1)}, u32[]{:S(2)}, u32[]{:S(2)}) collective-permute-start(f32[6,96,128]{2,1,0:T(8,128)S(1)} %slice.5), channel_id=1, source_target_pairs={{0,2},{2,4},{4,6},{6,8},{8,10},{10,12},{12,14},{14,16},{16,18},{18... | collective-permute-start | bytes 884744 | tf_op jit(solution)/shard_map/ppermute | solution.py:605
  16.0 0.0 copy-start
  16.0 0.6 %copy-done = s32[3]{0:T(128)S(1)} copy-done((s32[3]{0:T(128)S(1)}, s32[3]{0:T(128)}, u32[]{:S(2)}) %copy-start) | copy-done | bytes 36
  16.7 0.6 %factors.1 = (f32[4,96,128]{2,1,0:T(8,128)S(1)}, f32[35,8,128]{2,1,0:T(8,128)S(1)}) custom-call(s32[3]{0:T(128)S(1)} %copy-done, f32[1]{0:T(128)S(6)} %copy.8.refs_1_, s32[1]{0:T(128)S(6)} %copy.9.refs_2_, s32[1]{0:T(128)} %bitcast.3.refs_3_), custom_call_target="tpu_custom_call" | custom-call | bytes 1 | tf_op jit(solution)/shard_map/factors/pallas_call | solution.py:567
  17.3 0.0 collective-permute-done.1.refs_2_.refs_1_
  17.4 0.8 %apply_core.1.refs_3_ = f32[2,2,2,96,128]{4,3,2,1,0:T(8,128)S(1)} custom-call(f32[9,96,128]{2,1,0:T(8,128)S(1)} %pad_maximum_fusion.refs_0_.refs_1_, f32[9,96,128]{2,1,0:T(8,128)S(1)} %collective-permute-done.2.refs_1_, f32[6,96,128]{2,1,0:T(8,128)S(1)} %collective-permute-done.3.refs_2_, ...), custom_call_target="tpu_custom_call" | custom-call | bytes 1 | tf_op jit(solution)/shard_map/apply_core/pallas_call | solution.py:567
  18.2 0.8 %apply_own.1 = (f32[2,2,2,96,128]{4,3,2,1,0:T(8,128)S(1)}, f32[2,2,96,128]{3,2,1,0:T(8,128)S(1)}, f32[2,2,2,96,128]{4,3,2,1,0:T(8,128)S(1)}) custom-call(f32[9,96,128]{2,1,0:T(8,128)S(1)} %pad_maximum_fusion.refs_0_.refs_1_, f32[9,96,128]{2,1,0:T(8,128)S(1)} %collective-permute-done.2.refs_1_, ...), custom_call_target="tpu_custom_call" | custom-call | bytes 1 | tf_op jit(solution)/shard_map/apply_own/pallas_call | solution.py:567
  19.1 0.9 %apply_side.1 = (f32[2,2,2,96,128]{4,3,2,1,0:T(8,128)S(1)}, f32[2,2,96,128]{3,2,1,0:T(8,128)S(1)}, f32[2,2,2,96,128]{4,3,2,1,0:T(8,128)S(1)}) custom-call(f32[9,96,128]{2,1,0:T(8,128)S(1)} %pad_maximum_fusion.refs_0_.refs_1_, f32[9,96,128]{2,1,0:T(8,128)S(1)} %collective-permute-done.refs_2_.refs_1_.refs_0_, ...), custom_call_target="tpu_custom_call" | custom-call | bytes 1 | tf_op jit(solution)/shard_map/apply_side/pallas_call | solution.py:567
  19.9 1.0 %apply_second.1 = (f32[2,2,2,96,128]{4,3,2,1,0:T(8,128)S(1)}, f32[2,2,96,128]{3,2,1,0:T(8,128)S(1)}, f32[2,2,2,96,128]{4,3,2,1,0:T(8,128)S(1)}) custom-call(f32[9,96,128]{2,1,0:T(8,128)S(1)} %pad_maximum_fusion.refs_0_.refs_1_, f32[2,2,2,96,128]{4,3,2,1,0:T(8,128)S(1)} %get-tuple-element.26.refs_1_.refs_2_, ...), custom_call_target="tpu_custom_call" | custom-call | bytes 1 | tf_op jit(solution)/shard_map/apply_second/pallas_call | solution.py:567
  20.9 3.4 %collective-permute-start.4 = (f32[2,2,2,96,128]{4,3,2,1,0:T(8,128)S(1)}, f32[2,2,2,96,128]{4,3,2,1,0:T(8,128)S(1)}, u32[]{:S(2)}, u32[]{:S(2)}) collective-permute-start(f32[2,2,2,96,128]{4,3,2,1,0:T(8,128)S(1)} %get-tuple-element.34), channel_id=1, source_target_pairs={{0,1},{1,0},{2,3},{3,2},{4,5},{5,4},{6,7},{7,6},{8,9},{9,8},{10,11... | collective-permute-start | bytes 1179656 | tf_op jit(solution)/shard_map/ppermute | solution.py:608
  24.3 2.9 %apply_behind.1.refs_7_ = f32[2,2,2,96,128]{4,3,2,1,0:T(8,128)S(1)} custom-call(f32[9,96,128]{2,1,0:T(8,128)S(1)} %collective-permute-done.refs_2_.refs_1_.refs_0_, f32[9,96,128]{2,1,0:T(8,128)S(1)} %collective-permute-done.1.refs_2_.refs_1_, f32[6,96,128]{2,1,0:T(8,128)S(1)} %collective-permute-done.5.refs_2_, ...), custom_call_target="tpu_custom_call" | custom-call | flops 68719476736 | bytes 134217728 | tf_op jit(solution)/shard_map/apply_behind/pallas_call | solution.py:567
  27.3 0.2 sums.1.refs_0_
  27.5 0.5 products.1
  28.0 1.1 %apply_third.1 = f32[64,128]{1,0:T(8,128)S(1)} custom-call(f32[1,128]{1,0:T(1,128)S(1)} %get-tuple-element.33.refs_0_, f32[9,96,128]{2,1,0:T(8,128)S(1)} %pad_maximum_fusion.refs_0_.refs_1_, f32[2,2,2,96,128]{4,3,2,1,0:T(8,128)S(1)} %get-tuple-element.26.refs_1_.refs_2_, f32[2,2,96,128]{3,2,1,0:T(8,128)S(1)} %get-tuple-element.27.refs_2_.refs_3_, ...), custom_call_target="tpu_custom_call" | custom-call | bytes 1 | tf_op jit(solution)/shard_map/apply_third/pallas_call | solution.py:567
  29.1 21.0 %all_to_all.16 = f32[64,1,128]{2,1,0:T(1,128)S(1)} all-to-all(f32[64,1,128]{2,1,0:T(1,128)S(1)} %bitcast.9), channel_id=1, replica_groups=mesh['wl'=4,'gz'=64] {'gz'}, dimensions={0} | all-to-all | bytes 65536 | tf_op jit(solution)/shard_map/all_to_all | solution.py:689
  50.1 0.3 gradient.1
  50.4 8.4 %all_to_all.17 = f32[4,24,128]{2,1,0:T(8,128)S(1)} all-to-all(f32[4,24,128]{2,1,0:T(8,128)S(1)} %gradient.1), channel_id=1, replica_groups=mesh['wl'=4,'gz'=64] {'wl'}, dimensions={0} | all-to-all | bytes 98304 | tf_op jit(solution)/shard_map/all_to_all | solution.py:698
  58.7 0.6 %reduce_sum.9 = f32[24,128]{1,0:T(8,128)} reduce(f32[4,24,128]{2,1,0:T(8,128)S(1)} %all_to_all.17, f32[]{:T(128)} %constant.1.clone.1), dimensions={0}, to_apply=%region_0.0 | reduce | flops 9216 | bytes 61444 | tf_op jit(solution)/shard_map/reduce_sum | solution.py:699
  (5 shorter events, 0.0 us)
Async XLA Ops:
  1.1 12.2 %collective-permute-start = (f32[9,96,128]{2,1,0:T(8,128)S(1)}, f32[9,96,128]{2,1,0:T(8,128)S(1)}, u32[]{:S(2)}, u32[]{:S(2)}) collective-permute-start(f32[9,96,128]{2,1,0:T(8,128)S(1)} %pad_maximum_fusion.refs_0_.refs_1_), channel_id=1, source_target_pairs={{1,2},{2,1},{3,4},{4,3},{5,6},{6,5},{7,8},{8,7},{9,10},{10,9},{11,... | collective-permute-start | bytes 1327112 | tf_op jit(solution)/shard_map/ppermute | solution.py:610
  6.0 11.3 %collective-permute-start.2 = (f32[9,96,128]{2,1,0:T(8,128)S(1)}, f32[9,96,128]{2,1,0:T(8,128)S(1)}, u32[]{:S(2)}, u32[]{:S(2)}) collective-permute-start(f32[9,96,128]{2,1,0:T(8,128)S(1)} %pad_maximum_fusion.refs_0_.refs_1_), channel_id=1, source_target_pairs={{0,1},{1,0},{2,3},{3,2},{4,5},{5,4},{6,7},{7,6},{8,9},{9,8},{10,11... | collective-permute-start | bytes 1327112 | tf_op jit(solution)/shard_map/ppermute | solution.py:608
  6.1 11.2 %collective-permute-start.1 = (f32[9,96,128]{2,1,0:T(8,128)S(1)}, f32[9,96,128]{2,1,0:T(8,128)S(1)}, u32[]{:S(2)}, u32[]{:S(2)}) collective-permute-start(f32[9,96,128]{2,1,0:T(8,128)S(1)} %pad_maximum_fusion.refs_0_.refs_1_), channel_id=1, source_target_pairs={{0,2},{2,4},{4,6},{6,8},{8,10},{10,12},{12,14},{14,16},{16,18},{18... | collective-permute-start | bytes 1327112 | tf_op jit(solution)/shard_map/ppermute | solution.py:605
  13.3 4.0 %collective-permute-start.3 = (f32[6,96,128]{2,1,0:T(8,128)S(1)}, f32[6,96,128]{2,1,0:T(8,128)S(1)}, u32[]{:S(2)}, u32[]{:S(2)}) collective-permute-start(f32[6,96,128]{2,1,0:T(8,128)S(1)} %slice.5), channel_id=1, source_target_pairs={{0,1},{1,0},{2,3},{3,2},{4,5},{5,4},{6,7},{7,6},{8,9},{9,8},{10,11... | collective-permute-start | bytes 884744 | tf_op jit(solution)/shard_map/ppermute | solution.py:608
  13.4 10.9 %collective-permute-start.5 = (f32[6,96,128]{2,1,0:T(8,128)S(1)}, f32[6,96,128]{2,1,0:T(8,128)S(1)}, u32[]{:S(2)}, u32[]{:S(2)}) collective-permute-start(f32[6,96,128]{2,1,0:T(8,128)S(1)} %slice.5), channel_id=1, source_target_pairs={{0,2},{2,4},{4,6},{6,8},{8,10},{10,12},{12,14},{14,16},{16,18},{18... | collective-permute-start | bytes 884744 | tf_op jit(solution)/shard_map/ppermute | solution.py:605
  16.0 0.7 %copy-start = (s32[3]{0:T(128)S(1)}, s32[3]{0:T(128)}, u32[]{:S(2)}) copy-start(s32[3]{0:T(128)} %refs_0_.1) | copy-start | bytes 40
  20.9 7.1 %collective-permute-start.4 = (f32[2,2,2,96,128]{4,3,2,1,0:T(8,128)S(1)}, f32[2,2,2,96,128]{4,3,2,1,0:T(8,128)S(1)}, u32[]{:S(2)}, u32[]{:S(2)}) collective-permute-start(f32[2,2,2,96,128]{4,3,2,1,0:T(8,128)S(1)} %get-tuple-element.34), channel_id=1, source_target_pairs={{0,1},{1,0},{2,3},{3,2},{4,5},{5,4},{6,7},{7,6},{8,9},{9,8},{10,11... | collective-permute-start | bytes 1179656 | tf_op jit(solution)/shard_map/ppermute | solution.py:608

commit v3 on v2

--- a/solution.py
+++ b/solution.py
@@ -8,6 +8,7 @@
 SIGMA_MAX = 1.0
 SHIFT = (0.0, 6.0, 12.0)
 ROWS = 8
+WIDEST = 4
 LANES = 128
 GRAM = [(0, 0), (0, 1), (1, 1), (0, 2), (1, 2), (2, 2), (0, 3), (1, 3), (2, 3), (3, 3)]
 PRODUCTS = [(i, j) for i in range(3) for j in range(3)]
@@ -15,6 +16,8 @@
 
 
 def cmul(a, b):
+    if a is None:
+        return b
     return a[0] * b[0] - a[1] * b[1], a[0] * b[1] + a[1] * b[0]
 
 
@@ -23,7 +26,13 @@
 
 
 def csub(a, b):
-    return a[0] - b[0], a[1] - b[1]
+    return minus(a[0], b[0]), minus(a[1], b[1])
+
+
+def minus(a, b):
+    if isinstance(b, float):
+        return a
+    return -b if isinstance(a, float) else a - b
 
 
 def cdiv(upper, lower):
@@ -75,7 +84,7 @@
     wx = widths[0].astype(jnp.float32)
     wy = widths[1].astype(jnp.float32)
     wz = widths[2].astype(jnp.float32)
-    slab = place[0]
+    slab = lax.rem(place[0], total_planes)
     for s in range(rows_x // ROWS):
         pos = (rowids() + s * ROWS).astype(jnp.float32)
         at = pl.ds(s * ROWS, ROWS)
@@ -88,7 +97,7 @@
     fv[5] = jnp.broadcast_to((slab % 2).astype(jnp.float32), (ROWS, LANES))
     fv[6] = jnp.broadcast_to(mask[0].astype(jnp.float32), (ROWS, LANES))
     side = 1 - 2 * (slab % 2)
-    for n, at_plane in enumerate((slab, slab - side, slab - 2 * side, slab + side)):
+    for n, at_plane in enumerate((slab, slab - side, slab - 2 * side)):
         plane = jnp.broadcast_to(at_plane.astype(jnp.float32), (ROWS, LANES))
         low = 7 + 7 * n
         fv[low], fv[low + 1] = profile(plane + 0.5, total_planes, wz, angular)
@@ -99,10 +108,13 @@
         fv[low + 5] = jnp.where(above_floor, below_im, 0.0)
         inside = (plane >= 0.0) & (plane < total_planes)
         fv[low + 6] = jnp.where(inside, 1.0, 0.0)
-
-
-OWN, CHIP, BEHIND, CORE = 0, 1, 2, 3
-FACTOR_BLOCKS = 35
+    for at, low in ((28, 14), (30, 21)):
+        way = cmul((fv[low], fv[low + 1]), (fv[low + 2], fv[low + 3]))
+        fv[at], fv[at + 1] = way[0] * fv[low + 6], way[1] * fv[low + 6]
+
+
+OWN, CHIP, BEHIND = 0, 1, 2
+FACTOR_BLOCKS = 32
 
 
 class Factors:
@@ -119,6 +131,8 @@
         self.fx = fx
 
     def x(self, s):
+        if s * ROWS >= WIDEST and s * ROWS + ROWS - 0.5 <= self.fx.shape[1] - 1 - WIDEST:
+            return None, None
         at = pl.ds(s * ROWS, ROWS)
         return (self.fx[0, at, :], self.fx[1, at, :]), (self.fx[2, at, :], self.fx[3, at, :])
 
@@ -133,6 +147,8 @@
 
 
 def rmul(factor, real):
+    if factor is None:
+        return real, 0.0
     return factor[0] * real, factor[1] * real
 
 
@@ -170,7 +186,8 @@
     curls = curl_of(fac, sh, xe, hx, hy, hz, hx_b, hy_b, before)
     out = []
     for c, e in enumerate((ex, ey, ez)):
-        out.append((curls[c][0] - fac.weight * eps(c, at) * e, curls[c][1]))
+        diagonal = 0.0 if eps is None else fac.weight * eps(c, at) * e
+        out.append((curls[c][0] - diagonal, curls[c][1]))
     return out, (hy, hz)
 
 
@@ -198,8 +215,8 @@
     return lambda c, at: ref[3 * q + c, at, :]
 
 
-def eps_of(ref):
-    return lambda c, at: ref[6 + c, at, :]
+def eps_of(ref, first=6):
+    return lambda c, at: ref[first + c, at, :]
 
 
 def either(mask, yes, no):
@@ -215,7 +232,7 @@
 
 
 def side_of(ref, q):
-    return lambda c, at: (ref[c, q, 0, at, :], ref[c, q, 1, at, :])
+    return lambda c, at: tuple(part_of(ref, c)[q, p, at, :] for p in range(2))
 
 
 def either_pair(mask, yes, no):
@@ -223,6 +240,10 @@
         return tuple(jnp.where(mask, a, b) for a, b in zip(yes(c, at), no(c, at)))
 
     return read
+
+
+def part_of(ref, c):
+    return ref[c] if isinstance(ref, tuple) else ref.at[c]
 
 
 def store_sends(fac, sh, field, ez_n, q, s, sc, sz):
@@ -237,7 +258,7 @@
     for c, (down, above) in enumerate(((ex, part_x), (ey, part_y))):
         for p in range(2):
             if sc is not None:
-                sc[c, q, p, at, :] = jnp.where(fac.upper_core, down[p], above[p])
+                part_of(sc, c)[q, p, at, :] = jnp.where(fac.upper_core, down[p], above[p])
             if sz is not None:
                 sz[c, q, p, at, :] = jnp.where(fac.upper_core, above[p], down[p])
 
@@ -289,7 +310,12 @@
     return [tuple(v * fac.inside for v in pair) for pair in field]
 
 
-def own_kernel(strips, x, ca, za, fx, fv, uxy, uz, sz):
+def pack_kernel(sources, eps, out):
+    out[0:6] = sources[0:6]
+    out[6:9] = eps[6:9]
+
+
+def own_kernel(strips, x, ca, za, fx, fv, uxy, uz, scx, scy, sz):
     fac, sh = Factors(fv, fx), Shifts()
     core = fac.upper_core
     for q in range(2):
@@ -303,7 +329,7 @@
 
             real_strips(fac, sh, lo, plane_of(x, q), hi, eps_of(x), strips, both)
 
-        with_sends(fac, sh, q, strips, None, sz, run)
+        with_sends(fac, sh, q, strips, (scx, scy), sz, run)
 
 
 def side_kernel(strips, x, za, zb, fx, fv, uxy, uz, rz):
@@ -319,25 +345,12 @@
                 store_field(field, q, s, uxy, uz)
                 store(field, s)
 
-            real_strips(fac, sh, lo, plane_of(za, q), hi, eps_of(za), strips, both)
+            real_strips(fac, sh, lo, plane_of(za, q), hi, eps_of(zb), strips, both)
 
         with_sends(fac, sh, q, strips, rz, None, run)
 
 
-def core_kernel(strips, x, ca, cb, fx, fv, rc):
-    fac, sh = Factors(fv, fx, CORE), Shifts()
-    core = fac.upper_core
-    for q in range(2):
-        hi = either(core, plane_of(x, q), plane_of(cb, q))
-        lo = either(core, plane_of(cb, q), plane_of(x, q))
-
-        def run(store):
-            real_strips(fac, sh, lo, plane_of(ca, q), hi, eps_of(ca), strips, store)
-
-        with_sends(fac, sh, q, strips, None, rc, run)
-
-
-def second_kernel(strips, x, u1xy, u1z, rc, rz, fx, fv, uxy, uz, sc):
+def second_kernel(strips, x, u1xy, u1z, rcx, rcy, rz, fx, fv, uxy, uz, sc):
     fac, sh = Factors(fv, fx), Shifts()
     for q in range(2):
 
@@ -347,35 +360,73 @@
                 store(field, s)
 
             complex_strips(
-                fac, sh, eps_of(x), u1xy, u1z, rc, rz, q, strips, SHIFT[1], both
+                fac, sh, eps_of(x), u1xy, u1z, (rcx, rcy), rz, q, strips, SHIFT[1], both
             )
 
         with_sends(fac, sh, q, strips, sc, None, run)
 
 
-def behind_kernel(strips, za, zb, zc, sz, side_xy, side_z, fx, fv, rz2, rz1):
-    sh = Shifts()
+def behind_kernel(strips, za, zb, fx, fv, rz):
+    fac, sh = Factors(fv, fx, BEHIND), Shifts()
+    core = fac.upper_core
     for q in range(2):
-        fac = Factors(fv, fx, BEHIND)
-        core = fac.upper_core
-        hi = either(core, plane_of(zc, q), plane_of(za, q))
-        lo = either(core, plane_of(za, q), plane_of(zc, q))
-
-        def run_first(store):
+        near = plane_of(za, q)
+        hi = lambda c, at: jnp.where(core, 0.0, near(c, at))
+        lo = lambda c, at: jnp.where(core, near(c, at), 0.0)
+
+        def run(store):
             masked_store = lambda field, s: store(masked(fac, field), s)
-            real_strips(fac, sh, lo, plane_of(zb, q), hi, eps_of(zb), strips, masked_store)
-
-        with_sends(fac, sh, q, strips, rz1, None, run_first)
+            real_strips(fac, sh, lo, plane_of(zb, q), hi, None, strips, masked_store)
+
+        with_sends(fac, sh, q, strips, rz, None, run)
+
+
+def side_second_kernel(strips, zb, rz, sz, side_xy, side_z, fx, fv, out):
+    fac, sh = Factors(fv, fx, CHIP), Shifts()
     for q in range(2):
-        fac = Factors(fv, fx, CHIP)
-
-        def run_second(store):
+
+        def run(store):
             masked_store = lambda field, s: store(masked(fac, field), s)
             complex_strips(
-                fac, sh, eps_of(za), side_xy, side_z, sz, rz1, q, strips, SHIFT[1], masked_store
+                fac, sh, eps_of(zb), side_xy, side_z, sz, rz, q, strips, SHIFT[1], masked_store
             )
 
-        with_sends(fac, sh, q, strips, rz2, None, run_second)
+        with_sends(fac, sh, q, strips, out, None, run)
+
+
+def halo_form(fac, sh, zh, s, fields, ez_n):
+    ex, ey, ez = fields
+    xh, _ = fac.x(s)
+    part_x = cadd(rmul(fac.yh, sh.y_next(ez) - ez), rmul(zh, ey))
+    part_y = csub(rmul(zh, -ex), rmul(xh, sh.x_next(ez, ez_n) - ez))
+    return [
+        (jnp.where(fac.upper_core, down, above[0]), jnp.where(fac.upper_core, 0.0, above[1]))
+        for down, above in ((ex, part_x), (ey, part_y))
+    ]
+
+
+def far_kernel(strips, rz, zb, zc, fx, fv, out):
+    fac, sh = Factors(fv, fx, BEHIND), Shifts()
+    near_way, far_way = (fv[28], fv[29]), (fv[30], fv[31])
+    for q in range(2):
+
+        def scaled(c, at):
+            return zc[6 + c, at, :] * zb[3 * q + c, at, :]
+
+        def far(c, at):
+            return zc[3 * q + c, at, :]
+
+        for s in range(strips):
+            at = here(s)
+            forms = []
+            for read, zh in ((scaled, fac.zh), (far, fac.zb)):
+                ez_n = zeros() if s + 1 == strips else read(2, here(s + 1))
+                forms.append(halo_form(fac, sh, zh, s, [read(c, at) for c in range(3)], ez_n))
+            for c in range(2):
+                diagonal = (fac.weight * forms[0][c][0], fac.weight * forms[0][c][1])
+                change = cmul(near_way, cadd(diagonal, cmul(far_way, forms[1][c])))
+                for p in range(2):
+                    out[c, q, p, at, :] = rz[c, q, p, at, :] + change[p]
 
 
 def third_kernel(strips, before, x, u1xy, u1z, u2xy, u2z, rc, rz, fx, fv, row):
@@ -485,7 +536,7 @@
             return b
         return a if b is None else cadd(a, b)
 
-    def minus(a, b):
+    def less(a, b):
         if b is None:
             return a
         return (-b[0], -b[1]) if a is None else csub(a, b)
@@ -516,7 +567,7 @@
         solution = [plus(a, b) for a, b in zip(solution, scaled(step, direction))]
         if iteration == 2:
             break
-        residual = [minus(a, b) for a, b in zip(residual, scaled(step, pushed))]
+        residual = [less(a, b) for a, b in zip(residual, scaled(step, pushed))]
         image = image_of(residual[:3])
         rho_next = form(residual, image)
         ratio = cdiv(rho_next, rho)
@@ -527,7 +578,7 @@
     return solution[:3]
 
 
-def gradient_kernel(strips, rows, products, fv, out):
+def gradient_kernel(strips, slabs, place, rows, products, fv, *outs):
     total = jnp.sum(rows[...], axis=0, keepdims=True)
     lane, sub = laneids(), rowids()
     spread = jnp.broadcast_to(total, (ROWS, LANES))
@@ -550,14 +601,16 @@
         weights.append(both[0] * scale)
         if (i, j) != (0, 0):
             weights.append(-both[1] * scale)
-    per_share = strips // out.shape[0]
-    for s in range(strips):
-        at = pl.ds(s * ROWS, ROWS)
-        value = None
-        for place, weight in enumerate(weights):
-            term = weight * products[place, at, :]
-            value = term if value is None else value + term
-        out[s // per_share, pl.ds((s % per_share) * ROWS, ROWS), :] = value
+    mine, shares = lax.div(place[0], slabs), len(outs)
+    for k, out in enumerate(outs):
+        theirs = lax.rem(mine + k, shares) * (strips // shares)
+        for s in range(strips // shares):
+            at = pl.ds(pl.multiple_of((theirs + s) * ROWS, ROWS), ROWS)
+            value = None
+            for n, weight in enumerate(weights):
+                term = weight * products[n, at, :]
+                value = term if value is None else value + term
+            out[here(s), :] = value
 
 
 def call(kernel, outs, *args, smem=0, name=None, flops=0, cost=1, scratch=()):
@@ -572,7 +625,7 @@
         scratch_shapes=[VM(s, jnp.float32) for s in scratch],
         name=name,
         cost_estimate=pl.CostEstimate(flops=flops, bytes_accessed=cost, transcendentals=0),
-        compiler_params=pltpu.CompilerParams(vmem_limit_bytes=32 * 1024 * 1024),
+        compiler_params=pltpu.CompilerParams(vmem_limit_bytes=12 * 1024 * 1024),
     )(*args)
 
 
@@ -594,7 +647,7 @@
         chip_pairs += [(i, i + 1), (i + 1, i)]
     behind_pairs = [(i, i + 2) for i in range(0, slabs - 2, 2)]
     behind_pairs += [(i, i - 2) for i in range(3, slabs, 2)]
-    place = lax.axis_index("gz").astype(jnp.int32).reshape(1)
+    place = lax.axis_index(("wl", "gz")).astype(jnp.int32).reshape(1)
     x = jnp.concatenate(
         [a.reshape(3, rows_x, rows_y) for a in (source_fwd, source_adj, permittivity)], axis=0
     )
@@ -607,12 +660,9 @@
     def core_swap(value):
         return lax.ppermute(value, "gz", core_pairs)
 
-    za = lax.ppermute(x, "gz", chip_pairs)
-    zb = behind(x)
+    x = lax.optimization_barrier(x)
     ca = core_swap(x)
-    cb = core_swap(za[:6])
-    zc = behind(za[:6])
-    za, zb, ca, cb = lax.optimization_barrier((za, zb, ca, cb))
+    za = lax.ppermute(x[:6], "gz", chip_pairs)
     fx, fv = call(
         partial(factor_kernel, slabs, rows_x),
         [(4, rows_x, rows_y), (FACTOR_BLOCKS, ROWS, LANES)],
@@ -623,10 +673,22 @@
         smem=4,
         name="factors",
     )
-    u1xy, u1z, sz = call(
-        partial(own_kernel, strips), [field, plain, field], x, ca, za, fx, fv, name="apply_own"
-    )
-    (rc,) = call(partial(core_kernel, strips), [field], x, ca, cb, fx, fv, name="apply_core")
+    ca, fx, fv = lax.optimization_barrier((ca, fx, fv))
+    (pack,) = call(pack_kernel, [(9, rows_x, rows_y)], x, ca, name="pack")
+    zb = behind(pack)
+    (relay,) = call(pack_kernel, [(9, rows_x, rows_y)], za, x, name="pack_relay")
+    zc = behind(relay)
+    u1xy, u1z, scx, scy, sz = call(
+        partial(own_kernel, strips),
+        [field, plain, plain, plain, field],
+        x,
+        ca,
+        za,
+        fx,
+        fv,
+        name="apply_own",
+    )
+    rcx, rcy = core_swap(scx), core_swap(scy)
     side_xy, side_z, rz = call(
         partial(side_kernel, strips), [field, plain, field], x, za, zb, fx, fv, name="apply_side"
     )
@@ -637,7 +699,8 @@
         x,
         u1xy,
         u1z,
-        rc,
+        rcx,
+        rcy,
         rz,
         fx,
         fv,
@@ -655,19 +718,29 @@
         u2z,
         name="products",
     )
+    sz, row, products = lax.optimization_barrier((sz, row, products))
+    (rz,) = call(partial(behind_kernel, strips), [field], za, zb, fx, fv, name="apply_behind")
     (rz,) = call(
-        partial(behind_kernel, strips),
+        partial(side_second_kernel, strips),
         [field],
-        za,
         zb,
-        zc,
+        rz,
         sz,
         side_xy,
         side_z,
         fx,
         fv,
-        name="apply_behind",
-        scratch=[field],
+        name="apply_side_second",
+    )
+    (rz,) = call(
+        partial(far_kernel, strips),
+        [field],
+        rz,
+        zb,
+        zc,
+        fx,
+        fv,
+        name="add_far",
         flops=1 << 36,
         cost=1 << 27,
     )
@@ -687,16 +760,20 @@
         name="apply_third",
     )
     rows = lax.all_to_all(rows, "gz", 0, 0)
-    (parts,) = call(
-        partial(gradient_kernel, strips),
-        [(shares, rows_x // shares, rows_y)],
+    parts = call(
+        partial(gradient_kernel, strips, slabs),
+        [(rows_x // shares, rows_y)] * shares,
+        place,
         rows,
         products,
         fv,
+        smem=1,
         name="gradient",
     )
-    parts = lax.all_to_all(parts, "wl", 0, 0)
-    return jnp.sum(parts, axis=0)[None]
+    total = parts[0]
+    for k in range(1, shares):
+        total = total + lax.ppermute(parts[k], "wl", [(i, (i + k) % shares) for i in range(shares)])
+    return total[None]
 
 
 def solution(mesh):

time: 59.6 us -> 53.5 us (0.90)
  blocking collectives: 29.4 us -> 21.4 us
  starting transfers between devices: 11.1 us -> 14.2 us
  Pallas kernels: 9.12 us -> 6.83 us
  waiting for transfers between devices: 5.9 us -> 7.06 us
    all_to_all x1 -> x0, blocking collectives: 8.37 us -> none  [body(): parts = lax.all_to_all(parts, 'wl', 0, 0)]
    pallas_call x10 -> x13, Pallas kernels: 9.12 us -> 6.83 us  [call(): pl.pallas_call(kernel, out_shape=shapes, in_specs=specs, out_specs=outs_s...]
    ppermute x3 -> x4, starting transfers between devices: 3.6 us -> 5.81 us  [core_swap(): return lax.ppermute(value, 'gz', core_pairs)]
    ppermute x2, waiting for transfers between devices: 0.01 us -> 1.74 us  [behind(): return lax.ppermute(value, 'gz', behind_pairs)]
    ppermute x1 -> x4, starting transfers between devices: 4.94 us -> 5.77 us  [the longest x3 3.85 us: body(): lax.ppermute(parts[k], 'wl', [(i, (i + k) % shares) for i in range(shares)])]
    reduce_sum x1 -> x0, other arithmetic: 0.61 us -> none  [body(): return jnp.sum(parts, axis=0)[None]]
    broadcast_in_dim x0 -> x1, other arithmetic: none -> 0.6 us  [body(): return total[None]]
    ppermute x1 -> x4, waiting for transfers between devices: 5.88 us -> 5.31 us  [the longest x3 3.14 us: body(): lax.ppermute(parts[k], 'wl', [(i, (i + k) % shares) for i in range(shares)])]
  transfers between devices with their start and end apart: 6 -> 10, of which waited for: 1 -> 5; matrix products, arithmetic and copies ran while one was open for 0% -> 0% of each run, Pallas kernels for 13% -> 11%
where the time goes in v3:
time: 53.5 us; the launch traced here: 53.3 us
  blocking collectives  21.4 us (40%)
  starting transfers between devices  14.2 us (27%)
  waiting for transfers between devices  7.06 us (13%)
  Pallas kernels  6.83 us (13%)
  other arithmetic  1.69 us (3%)
  between operations  1.45 us (3%)
  local copies, waits for them, and re-layouts  0.67 us (1%)
    all_to_all x1, blocking collectives, body(): rows = lax.all_to_all(rows, 'gz', 0, 0)  21.4 us
    pallas_call x13, Pallas kernels, call(): pl.pallas_call(kernel, out_shape=shapes, in_specs=specs, out_specs=outs_s...  6.83 us
    ppermute x4, starting transfers between devices, core_swap(): return lax.ppermute(value, 'gz', core_pairs)  5.81 us
    ppermute x3, starting transfers between devices, body(): lax.ppermute(parts[k], 'wl', [(i, (i + k) % shares) for i in range(shares)])  3.85 us
    ppermute x3, waiting for transfers between devices, body(): lax.ppermute(parts[k], 'wl', [(i, (i + k) % shares) for i in range(shares)])  3.14 us
    ppermute x2, starting transfers between devices, behind(): return lax.ppermute(value, 'gz', behind_pairs)  2.58 us
    ppermute x1, waiting for transfers between devices, body(): za = lax.ppermute(x[:6], 'gz', chip_pairs)  2.17 us
    ppermute x1, starting transfers between devices, body(): za = lax.ppermute(x[:6], 'gz', chip_pairs)  1.92 us
  transfers between devices with their start and end apart: 10, of which 5 were waited for; matrix products, arithmetic and copies ran while one was open for 0% of the time, Pallas kernels for 11%

profile of v3, /device:TPU:1, one launch (start us, length us, event | category | flops | bytes accessed | tf_op | source)
XLA Modules:
  0.0 53.3 jit_solution(14951186439267878770)
XLA Ops:
  0.0 1.1 %pad_maximum_fusion.refs_0_.sources.refs_1_.eps = f32[9,96,128]{2,1,0:T(8,128)S(1)} fusion(f32[3,96,128]{2,1,0:T(8,128)} %bitcast.12, f32[3,96,128]{2,1,0:T(8,128)} %bitcast.13, f32[3,96,128]{2,1,0:T(8,128)} %bitcast.14), kind=kLoop, calls=%fused_computation | loop fusion | flops 221184 | bytes 884736 | tf_op jit(solution)/shard_map/concatenate | solution.py:651
  1.1 3.3 %collective-permute-start = (f32[9,96,128]{2,1,0:T(8,128)S(1)}, f32[9,96,128]{2,1,0:T(8,128)S(1)}, u32[]{:S(2)}, u32[]{:S(2)}) collective-permute-start(f32[9,96,128]{2,1,0:T(8,128)S(1)} %pad_maximum_fusion.refs_0_.sources.refs_1_.eps), channel_id=1, source_target_pairs={{0,1},{1,0},{2,3},{3,2},{4,5},{5,4},{6,7},{7,6},{8,9},{9,8},{10,11... | collective-permute-start | bytes 1327112 | tf_op jit(solution)/shard_map/ppermute | solution.py:661
  4.4 1.9 %collective-permute-start.1 = (f32[6,96,128]{2,1,0:T(8,128)S(1)}, f32[6,96,128]{2,1,0:T(8,128)S(1)}, u32[]{:S(2)}, u32[]{:S(2)}) collective-permute-start(f32[6,96,128]{2,1,0:T(8,128)S(1)} %slice.4), channel_id=1, source_target_pairs={{1,2},{2,1},{3,4},{4,3},{5,6},{6,5},{7,8},{8,7},{9,10},{10,9},{11,... | collective-permute-start | bytes 884744 | tf_op jit(solution)/shard_map/ppermute | solution.py:665
  7.7 0.6 %copy-done = s32[3]{0:T(128)S(1)} copy-done((s32[3]{0:T(128)S(1)}, s32[3]{0:T(128)}, u32[]{:S(2)}) %copy-start) | copy-done | bytes 36
  8.3 0.6 %factors.1 = (f32[4,96,128]{2,1,0:T(8,128)S(1)}, f32[32,8,128]{2,1,0:T(8,128)S(1)}) custom-call(s32[3]{0:T(128)S(1)} %copy-done, f32[1]{0:T(128)S(6)} %copy.8.refs_1_, s32[1]{0:T(128)S(6)} %copy.9.refs_2_, s32[1]{0:T(128)} %bitcast.refs_3_.refs_0_), custom_call_target="tpu_custom_call" | custom-call | bytes 1 | tf_op jit(solution)/shard_map/factors/pallas_call | solution.py:620
  9.0 1.3 %collective-permute-start.4 = (f32[9,96,128]{2,1,0:T(8,128)S(1)}, f32[9,96,128]{2,1,0:T(8,128)S(1)}, u32[]{:S(2)}, u32[]{:S(2)}) collective-permute-start(f32[9,96,128]{2,1,0:T(8,128)S(1)} %pack.1), channel_id=1, source_target_pairs={{0,2},{2,4},{4,6},{6,8},{8,10},{10,12},{12,14},{14,16},{16,18},{18... | collective-permute-start | bytes 1327112 | tf_op jit(solution)/shard_map/ppermute | solution.py:658
  10.3 2.2 %collective-permute-done.1.refs_2_.refs_1_.refs_0_.sources = f32[6,96,128]{2,1,0:T(8,128)S(1)} collective-permute-done((f32[6,96,128]{2,1,0:T(8,128)S(1)}, f32[6,96,128]{2,1,0:T(8,128)S(1)}, u32[]{:S(2)}, u32[]{:S(2)}) %collective-permute-start.1) | collective-permute-done | bytes 294944 | tf_op jit(solution)/shard_map/ppermute | solution.py:665
  12.5 1.3 %collective-permute-start.6 = (f32[9,96,128]{2,1,0:T(8,128)S(1)}, f32[9,96,128]{2,1,0:T(8,128)S(1)}, u32[]{:S(2)}, u32[]{:S(2)}) collective-permute-start(f32[9,96,128]{2,1,0:T(8,128)S(1)} %pack_relay.1), channel_id=1, source_target_pairs={{0,2},{2,4},{4,6},{6,8},{8,10},{10,12},{12,14},{14,16},{16,18},{18... | collective-permute-start | bytes 1327112 | tf_op jit(solution)/shard_map/ppermute | solution.py:658
  13.8 0.8 %apply_own.1 = (f32[2,2,2,96,128]{4,3,2,1,0:T(8,128)S(1)}, f32[2,2,96,128]{3,2,1,0:T(8,128)S(1)}, f32[2,2,96,128]{3,2,1,0:T(8,128)S(1)}, f32[2,2,96,128]{3,2,1,0:T(8,128)S(1)}, f32[2,2,2,96,128]{4,3,2,1,0:T(8,128)S(1)}) custom-call(f32[9,96,128]{2,1,0:T(8,128)S(1)} %pad_maximum_fusion.refs_0_.sources.refs_1_.eps, ...), custom_call_target="tpu_custom_call" | custom-call | bytes 1 | tf_op jit(solution)/shard_map/apply_own/pallas_call | solution.py:620
  14.6 1.5 %collective-permute-start.2 = (f32[2,2,96,128]{3,2,1,0:T(8,128)S(1)}, f32[2,2,96,128]{3,2,1,0:T(8,128)S(1)}, u32[]{:S(2)}, u32[]{:S(2)}) collective-permute-start(f32[2,2,96,128]{3,2,1,0:T(8,128)S(1)} %get-tuple-element.38), channel_id=1, source_target_pairs={{0,1},{1,0},{2,3},{3,2},{4,5},{5,4},{6,7},{7,6},{8,9},{9,8},{10,11... | collective-permute-start | bytes 589832 | tf_op jit(solution)/shard_map/ppermute | solution.py:661
  16.4 1.6 %collective-permute-done.4.refs_2_.refs_1_.refs_0_ = f32[9,96,128]{2,1,0:T(8,128)S(1)} collective-permute-done((f32[9,96,128]{2,1,0:T(8,128)S(1)}, f32[9,96,128]{2,1,0:T(8,128)S(1)}, u32[]{:S(2)}, u32[]{:S(2)}) %collective-permute-start.4) | collective-permute-done | bytes 442400 | tf_op jit(solution)/shard_map/ppermute | solution.py:658
  18.1 0.8 %apply_side.1 = (f32[2,2,2,96,128]{4,3,2,1,0:T(8,128)S(1)}, f32[2,2,96,128]{3,2,1,0:T(8,128)S(1)}, f32[2,2,2,96,128]{4,3,2,1,0:T(8,128)S(1)}) custom-call(f32[9,96,128]{2,1,0:T(8,128)S(1)} %pad_maximum_fusion.refs_0_.sources.refs_1_.eps, f32[6,96,128]{2,1,0:T(8,128)S(1)} %collective-permute-done.1.refs_2_.refs_1_.refs_0_.sources, ...), custom_call_target="tpu_custom_call" | custom-call | bytes 1 | tf_op jit(solution)/shard_map/apply_side/pallas_call | solution.py:620
  18.8 0.9 %apply_second.1 = (f32[2,2,2,96,128]{4,3,2,1,0:T(8,128)S(1)}, f32[2,2,96,128]{3,2,1,0:T(8,128)S(1)}, f32[2,2,2,96,128]{4,3,2,1,0:T(8,128)S(1)}) custom-call(f32[9,96,128]{2,1,0:T(8,128)S(1)} %pad_maximum_fusion.refs_0_.sources.refs_1_.eps, f32[2,2,2,96,128]{4,3,2,1,0:T(8,128)S(1)} %get-tuple-element.36.refs_1_.refs_2_, ...), custom_call_target="tpu_custom_call" | custom-call | bytes 1 | tf_op jit(solution)/shard_map/apply_second/pallas_call | solution.py:620
  19.8 0.5 products.1
  20.2 0.9 %collective-permute-start.5 = (f32[2,2,2,96,128]{4,3,2,1,0:T(8,128)S(1)}, f32[2,2,2,96,128]{4,3,2,1,0:T(8,128)S(1)}, u32[]{:S(2)}, u32[]{:S(2)}) collective-permute-start(f32[2,2,2,96,128]{4,3,2,1,0:T(8,128)S(1)} %get-tuple-element.46), channel_id=1, source_target_pairs={{0,1},{1,0},{2,3},{3,2},{4,5},{5,4},{6,7},{7,6},{8,9},{9,8},{10,11... | collective-permute-start | bytes 1179656 | tf_op jit(solution)/shard_map/ppermute | solution.py:661
  21.1 0.8 %apply_behind.1.refs_1_ = f32[2,2,2,96,128]{4,3,2,1,0:T(8,128)S(1)} custom-call(f32[6,96,128]{2,1,0:T(8,128)S(1)} %collective-permute-done.1.refs_2_.refs_1_.refs_0_.sources, f32[9,96,128]{2,1,0:T(8,128)S(1)} %collective-permute-done.4.refs_2_.refs_1_.refs_0_, f32[4,96,128]{2,1,0:T(8,128)S(1)} %get-tuple-element.33.refs_3_.refs_6_.refs_2_.refs_5_.refs_8_, ...), custom_call_target="tpu_custom_call" | custom-call | bytes 1 | tf_op jit(solution)/shard_map/apply_behind/pallas_call | solution.py:620
  21.9 0.8 %apply_side_second.1.refs_0_ = f32[2,2,2,96,128]{4,3,2,1,0:T(8,128)S(1)} custom-call(f32[9,96,128]{2,1,0:T(8,128)S(1)} %collective-permute-done.4.refs_2_.refs_1_.refs_0_, f32[2,2,2,96,128]{4,3,2,1,0:T(8,128)S(1)} %apply_behind.1.refs_1_, f32[2,2,2,96,128]{4,3,2,1,0:T(8,128)S(1)} %get-tuple-element.47.refs_2_, ...), custom_call_target="tpu_custom_call" | custom-call | bytes 1 | tf_op jit(solution)/shard_map/apply_side_second/pallas_call | solution.py:620
  23.1 0.9 %apply_third.1 = f32[64,128]{1,0:T(8,128)S(1)} custom-call(f32[1,128]{1,0:T(1,128)S(1)} %get-tuple-element.45.refs_0_, f32[9,96,128]{2,1,0:T(8,128)S(1)} %pad_maximum_fusion.refs_0_.sources.refs_1_.eps, f32[2,2,2,96,128]{4,3,2,1,0:T(8,128)S(1)} %get-tuple-element.36.refs_1_.refs_2_, f32[2,2,96,128]{3,2,1,0:T(8,128)S(1)} %get-tuple-element.37.refs_2_.refs_3_, ...), custom_call_target="tpu_custom_call" | custom-call | bytes 1 | tf_op jit(solution)/shard_map/apply_third/pallas_call | solution.py:620
  24.0 21.4 %all_to_all.11 = f32[64,1,128]{2,1,0:T(1,128)S(1)} all-to-all(f32[64,1,128]{2,1,0:T(1,128)S(1)} %bitcast.10), channel_id=1, replica_groups=mesh['wl'=4,'gz'=64] {'gz'}, dimensions={0} | all-to-all | bytes 65536 | tf_op jit(solution)/shard_map/all_to_all | solution.py:762
  45.7 2.8 %collective-permute-start.9 = (f32[24,128]{1,0:T(8,128)S(1)}, f32[24,128]{1,0:T(8,128)S(1)}, u32[]{:S(2)}, u32[]{:S(2)}) collective-permute-start(f32[24,128]{1,0:T(8,128)S(1)} %get-tuple-element.54), channel_id=1, source_target_pairs={{0,192},{64,0},{128,64},{192,128},{1,193},{65,1},{129,65},{193,129... | collective-permute-start | bytes 36872 | tf_op jit(solution)/shard_map/ppermute | solution.py:775
  48.5 0.3 collective-permute-start.8
  48.8 0.7 %collective-permute-start.7 = (f32[24,128]{1,0:T(8,128)S(1)}, f32[24,128]{1,0:T(8,128)S(1)}, u32[]{:S(2)}, u32[]{:S(2)}) collective-permute-start(f32[24,128]{1,0:T(8,128)S(1)} %get-tuple-element.52), channel_id=1, source_target_pairs={{0,64},{64,128},{128,192},{192,0},{1,65},{65,129},{129,193},{193,1... | collective-permute-start | bytes 36872 | tf_op jit(solution)/shard_map/ppermute | solution.py:775
  49.5 3.0 %collective-permute-done.8 = f32[24,128]{1,0:T(8,128)S(1)} collective-permute-done((f32[24,128]{1,0:T(8,128)S(1)}, f32[24,128]{1,0:T(8,128)S(1)}, u32[]{:S(2)}, u32[]{:S(2)}) %collective-permute-start.8) | collective-permute-done | bytes 12320 | tf_op jit(solution)/shard_map/ppermute | solution.py:775
  52.7 0.6 %add_bitcast_fusion = f32[1,24,128]{2,1,0:T(8,128)} fusion(f32[24,128]{1,0:T(8,128)S(1)} %collective-permute-done.9, f32[24,128]{1,0:T(8,128)S(1)} %collective-permute-done.8, f32[24,128]{1,0:T(8,128)S(1)} %get-tuple-element.51, f32[24,128]{1,0:T(8,128)S(1)} %collective-permute-done.7), kind=kLoop, calls=%fused_computation.1 | loop fusion | flops 9216 | bytes 61440 | tf_op jit(solution)/shard_map/broadcast_in_dim | solution.py:776
  (15 shorter events, 1.1 us)
Async XLA Ops:
  1.1 7.9 %collective-permute-start = (f32[9,96,128]{2,1,0:T(8,128)S(1)}, f32[9,96,128]{2,1,0:T(8,128)S(1)}, u32[]{:S(2)}, u32[]{:S(2)}) collective-permute-start(f32[9,96,128]{2,1,0:T(8,128)S(1)} %pad_maximum_fusion.refs_0_.sources.refs_1_.eps), channel_id=1, source_target_pairs={{0,1},{1,0},{2,3},{3,2},{4,5},{5,4},{6,7},{7,6},{8,9},{9,8},{10,11... | collective-permute-start | bytes 1327112 | tf_op jit(solution)/shard_map/ppermute | solution.py:661
  4.4 8.0 %collective-permute-start.1 = (f32[6,96,128]{2,1,0:T(8,128)S(1)}, f32[6,96,128]{2,1,0:T(8,128)S(1)}, u32[]{:S(2)}, u32[]{:S(2)}) collective-permute-start(f32[6,96,128]{2,1,0:T(8,128)S(1)} %slice.4), channel_id=1, source_target_pairs={{1,2},{2,1},{3,4},{4,3},{5,6},{6,5},{7,8},{8,7},{9,10},{10,9},{11,... | collective-permute-start | bytes 884744 | tf_op jit(solution)/shard_map/ppermute | solution.py:665
  7.7 0.7 %copy-start = (s32[3]{0:T(128)S(1)}, s32[3]{0:T(128)}, u32[]{:S(2)}) copy-start(s32[3]{0:T(128)} %refs_0_.1) | copy-start | bytes 40
  9.0 9.0 %collective-permute-start.4 = (f32[9,96,128]{2,1,0:T(8,128)S(1)}, f32[9,96,128]{2,1,0:T(8,128)S(1)}, u32[]{:S(2)}, u32[]{:S(2)}) collective-permute-start(f32[9,96,128]{2,1,0:T(8,128)S(1)} %pack.1), channel_id=1, source_target_pairs={{0,2},{2,4},{4,6},{6,8},{8,10},{10,12},{12,14},{14,16},{16,18},{18... | collective-permute-start | bytes 1327112 | tf_op jit(solution)/shard_map/ppermute | solution.py:658
  12.5 10.3 %collective-permute-start.6 = (f32[9,96,128]{2,1,0:T(8,128)S(1)}, f32[9,96,128]{2,1,0:T(8,128)S(1)}, u32[]{:S(2)}, u32[]{:S(2)}) collective-permute-start(f32[9,96,128]{2,1,0:T(8,128)S(1)} %pack_relay.1), channel_id=1, source_target_pairs={{0,2},{2,4},{4,6},{6,8},{8,10},{10,12},{12,14},{14,16},{16,18},{18... | collective-permute-start | bytes 1327112 | tf_op jit(solution)/shard_map/ppermute | solution.py:658
  14.6 4.2 %collective-permute-start.2 = (f32[2,2,96,128]{3,2,1,0:T(8,128)S(1)}, f32[2,2,96,128]{3,2,1,0:T(8,128)S(1)}, u32[]{:S(2)}, u32[]{:S(2)}) collective-permute-start(f32[2,2,96,128]{3,2,1,0:T(8,128)S(1)} %get-tuple-element.38), channel_id=1, source_target_pairs={{0,1},{1,0},{2,3},{3,2},{4,5},{5,4},{6,7},{7,6},{8,9},{9,8},{10,11... | collective-permute-start | bytes 589832 | tf_op jit(solution)/shard_map/ppermute | solution.py:661
  16.1 2.7 %collective-permute-start.3 = (f32[2,2,96,128]{3,2,1,0:T(8,128)S(1)}, f32[2,2,96,128]{3,2,1,0:T(8,128)S(1)}, u32[]{:S(2)}, u32[]{:S(2)}) collective-permute-start(f32[2,2,96,128]{3,2,1,0:T(8,128)S(1)} %get-tuple-element.39), channel_id=1, source_target_pairs={{0,1},{1,0},{2,3},{3,2},{4,5},{5,4},{6,7},{7,6},{8,9},{9,8},{10,11... | collective-permute-start | bytes 589832 | tf_op jit(solution)/shard_map/ppermute | solution.py:661
  20.2 2.8 %collective-permute-start.5 = (f32[2,2,2,96,128]{4,3,2,1,0:T(8,128)S(1)}, f32[2,2,2,96,128]{4,3,2,1,0:T(8,128)S(1)}, u32[]{:S(2)}, u32[]{:S(2)}) collective-permute-start(f32[2,2,2,96,128]{4,3,2,1,0:T(8,128)S(1)} %get-tuple-element.46), channel_id=1, source_target_pairs={{0,1},{1,0},{2,3},{3,2},{4,5},{5,4},{6,7},{7,6},{8,9},{9,8},{10,11... | collective-permute-start | bytes 1179656 | tf_op jit(solution)/shard_map/ppermute | solution.py:661
  45.7 3.9 %collective-permute-start.9 = (f32[24,128]{1,0:T(8,128)S(1)}, f32[24,128]{1,0:T(8,128)S(1)}, u32[]{:S(2)}, u32[]{:S(2)}) collective-permute-start(f32[24,128]{1,0:T(8,128)S(1)} %get-tuple-element.54), channel_id=1, source_target_pairs={{0,192},{64,0},{128,64},{192,128},{1,193},{65,1},{129,65},{193,129... | collective-permute-start | bytes 36872 | tf_op jit(solution)/shard_map/ppermute | solution.py:775
  48.5 4.1 %collective-permute-start.8 = (f32[24,128]{1,0:T(8,128)S(1)}, f32[24,128]{1,0:T(8,128)S(1)}, u32[]{:S(2)}, u32[]{:S(2)}) collective-permute-start(f32[24,128]{1,0:T(8,128)S(1)} %get-tuple-element.53), channel_id=1, source_target_pairs={{0,128},{64,192},{128,0},{192,64},{1,129},{65,193},{129,1},{193,65... | collective-permute-start | bytes 36872 | tf_op jit(solution)/shard_map/ppermute | solution.py:775
  48.8 3.8 %collective-permute-start.7 = (f32[24,128]{1,0:T(8,128)S(1)}, f32[24,128]{1,0:T(8,128)S(1)}, u32[]{:S(2)}, u32[]{:S(2)}) collective-permute-start(f32[24,128]{1,0:T(8,128)S(1)} %get-tuple-element.52), channel_id=1, source_target_pairs={{0,64},{64,128},{128,192},{192,0},{1,65},{65,129},{129,193},{193,1... | collective-permute-start | bytes 36872 | tf_op jit(solution)/shard_map/ppermute | solution.py:775

commit v4 on v3

--- a/solution.py
+++ b/solution.py
@@ -79,12 +79,10 @@
     return 1.0 / denominator, -ratios / denominator
 
 
-def factor_kernel(total_planes, rows_x, widths, omegas, mask, place, fx, fv):
-    angular = omegas[0]
-    wx = widths[0].astype(jnp.float32)
-    wy = widths[1].astype(jnp.float32)
-    wz = widths[2].astype(jnp.float32)
-    slab = lax.rem(place[0], total_planes)
+def factor_kernel(total_planes, rows_x, small, fx, fv):
+    angular, wx, wy, wz, mask, slab, upper = (
+        jnp.broadcast_to(small[:, n : n + 1], (ROWS, LANES)) for n in range(7)
+    )
     for s in range(rows_x // ROWS):
         pos = (rowids() + s * ROWS).astype(jnp.float32)
         at = pl.ds(s * ROWS, ROWS)
@@ -93,12 +91,11 @@
     pos = laneids().astype(jnp.float32)
     fv[0], fv[1] = profile(pos + 0.5, LANES, wy, angular)
     fv[2], fv[3] = profile(pos, LANES, wy, angular)
-    fv[4] = jnp.broadcast_to(angular * angular, (ROWS, LANES))
-    fv[5] = jnp.broadcast_to((slab % 2).astype(jnp.float32), (ROWS, LANES))
-    fv[6] = jnp.broadcast_to(mask[0].astype(jnp.float32), (ROWS, LANES))
-    side = 1 - 2 * (slab % 2)
-    for n, at_plane in enumerate((slab, slab - side, slab - 2 * side)):
-        plane = jnp.broadcast_to(at_plane.astype(jnp.float32), (ROWS, LANES))
+    fv[4] = angular * angular
+    fv[5] = upper
+    fv[6] = mask
+    side = 1.0 - 2.0 * upper
+    for n, plane in enumerate((slab, slab - side, slab - 2.0 * side)):
         low = 7 + 7 * n
         fv[low], fv[low + 1] = profile(plane + 0.5, total_planes, wz, angular)
         fv[low + 2], fv[low + 3] = profile(plane, total_planes, wz, angular)
@@ -312,7 +309,7 @@
 
 def pack_kernel(sources, eps, out):
     out[0:6] = sources[0:6]
-    out[6:9] = eps[6:9]
+    out[6:9] = eps[eps.shape[0] - 3 :]
 
 
 def own_kernel(strips, x, ca, za, fx, fv, uxy, uz, scx, scy, sz):
@@ -661,19 +658,18 @@
         return lax.ppermute(value, "gz", core_pairs)
 
     x = lax.optimization_barrier(x)
+    za = lax.ppermute(x[:6], "gz", chip_pairs)
     ca = core_swap(x)
-    za = lax.ppermute(x[:6], "gz", chip_pairs)
+    slab = lax.axis_index("gz")
+    numbers = [omegas, pml_widths, design_mask, slab.reshape(1), (slab % 2).reshape(1)]
+    small = jnp.concatenate([n.astype(jnp.float32) for n in numbers]).reshape(1, 7)
     fx, fv = call(
         partial(factor_kernel, slabs, rows_x),
         [(4, rows_x, rows_y), (FACTOR_BLOCKS, ROWS, LANES)],
-        pml_widths,
-        omegas,
-        design_mask,
-        place,
-        smem=4,
+        small,
         name="factors",
     )
-    ca, fx, fv = lax.optimization_barrier((ca, fx, fv))
+    ca, fx, fv, place = lax.optimization_barrier((ca, fx, fv, place))
     (pack,) = call(pack_kernel, [(9, rows_x, rows_y)], x, ca, name="pack")
     zb = behind(pack)
     (relay,) = call(pack_kernel, [(9, rows_x, rows_y)], za, x, name="pack_relay")

time: 53.5 us -> 53.3 us (level)
  waiting for transfers between devices: 7.06 us -> 7.78 us
  blocking collectives: 21.4 us -> 22 us
  starting transfers between devices: 14.2 us -> 13.6 us
  local copies, waits for them, and re-layouts: 0.67 us -> 0.11 us
    ppermute x1, waiting for transfers between devices: 2.17 us -> 3.22 us  [body(): za = lax.ppermute(x[:6], 'gz', chip_pairs)]
    unnamed x2, local copies, waits for them, and re-layouts: 0.65 us -> 0.01 us
    all_to_all x1, blocking collectives: 21.4 us -> 22 us  [body(): rows = lax.all_to_all(rows, 'gz', 0, 0)]
    ppermute x4, starting transfers between devices: 5.81 us -> 5.23 us  [core_swap(): return lax.ppermute(value, 'gz', core_pairs)]
  transfers between devices with their start and end apart: 10 -> 10, of which waited for: 5 -> 5; matrix products, arithmetic and copies ran while one was open for 0% -> 0% of each run, Pallas kernels for 11% -> 10%
where the time goes in v4:
time: 53.3 us; the launch traced here: 53 us
  blocking collectives  22 us (41%)
  starting transfers between devices  13.6 us (26%)
  waiting for transfers between devices  7.78 us (15%)
  Pallas kernels  6.36 us (12%)
  other arithmetic  1.69 us (3%)
  between operations  1.5 us (3%)
    all_to_all x1, blocking collectives, body(): rows = lax.all_to_all(rows, 'gz', 0, 0)  22 us
    pallas_call x13, Pallas kernels, call(): pl.pallas_call(kernel, out_shape=shapes, in_specs=specs, out_specs=outs_s...  6.36 us
    ppermute x4, starting transfers between devices, core_swap(): return lax.ppermute(value, 'gz', core_pairs)  5.23 us
    ppermute x3, starting transfers between devices, body(): lax.ppermute(parts[k], 'wl', [(i, (i + k) % shares) for i in range(shares)])  3.85 us
    ppermute x1, waiting for transfers between devices, body(): za = lax.ppermute(x[:6], 'gz', chip_pairs)  3.22 us
    ppermute x3, waiting for transfers between devices, body(): lax.ppermute(parts[k], 'wl', [(i, (i + k) % shares) for i in range(shares)])  3.14 us
    ppermute x2, starting transfers between devices, behind(): return lax.ppermute(value, 'gz', behind_pairs)  2.58 us
    ppermute x1, starting transfers between devices, body(): za = lax.ppermute(x[:6], 'gz', chip_pairs)  1.92 us
  transfers between devices with their start and end apart: 10, of which 5 were waited for; matrix products, arithmetic and copies ran while one was open for 0% of the time, Pallas kernels for 10%

profile of v4, /device:TPU:1, one launch (start us, length us, event | category | flops | bytes accessed | tf_op | source)
XLA Modules:
  0.0 53.0 jit_solution(338680182354821985)
XLA Ops:
  0.0 1.1 %pad_maximum_fusion.refs_0_.sources.refs_1_.eps = f32[9,96,128]{2,1,0:T(8,128)S(1)} fusion(f32[3,96,128]{2,1,0:T(8,128)} %bitcast.16, f32[3,96,128]{2,1,0:T(8,128)} %bitcast.17, f32[3,96,128]{2,1,0:T(8,128)} %bitcast.18), kind=kLoop, calls=%fused_computation | loop fusion | flops 221184 | bytes 884736 | tf_op jit(solution)/shard_map/concatenate | solution.py:648
  1.1 3.3 %collective-permute-start = (f32[9,96,128]{2,1,0:T(8,128)S(1)}, f32[9,96,128]{2,1,0:T(8,128)S(1)}, u32[]{:S(2)}, u32[]{:S(2)}) collective-permute-start(f32[9,96,128]{2,1,0:T(8,128)S(1)} %pad_maximum_fusion.refs_0_.sources.refs_1_.eps), channel_id=1, source_target_pairs={{0,1},{1,0},{2,3},{3,2},{4,5},{5,4},{6,7},{7,6},{8,9},{9,8},{10,11... | collective-permute-start | bytes 1327112 | tf_op jit(solution)/shard_map/ppermute | solution.py:658
  4.4 1.9 %collective-permute-start.1 = (f32[6,96,128]{2,1,0:T(8,128)S(1)}, f32[6,96,128]{2,1,0:T(8,128)S(1)}, u32[]{:S(2)}, u32[]{:S(2)}) collective-permute-start(f32[6,96,128]{2,1,0:T(8,128)S(1)} %slice.4), channel_id=1, source_target_pairs={{1,2},{2,1},{3,4},{4,3},{5,6},{6,5},{7,8},{8,7},{9,10},{10,9},{11,... | collective-permute-start | bytes 884744 | tf_op jit(solution)/shard_map/ppermute | solution.py:661
  8.0 1.3 %collective-permute-start.4 = (f32[9,96,128]{2,1,0:T(8,128)S(1)}, f32[9,96,128]{2,1,0:T(8,128)S(1)}, u32[]{:S(2)}, u32[]{:S(2)}) collective-permute-start(f32[9,96,128]{2,1,0:T(8,128)S(1)} %pack.1), channel_id=1, source_target_pairs={{0,2},{2,4},{4,6},{6,8},{8,10},{10,12},{12,14},{14,16},{16,18},{18... | collective-permute-start | bytes 1327112 | tf_op jit(solution)/shard_map/ppermute | solution.py:655
  9.3 3.2 %collective-permute-done.1.refs_2_.refs_1_.refs_0_.sources = f32[6,96,128]{2,1,0:T(8,128)S(1)} collective-permute-done((f32[6,96,128]{2,1,0:T(8,128)S(1)}, f32[6,96,128]{2,1,0:T(8,128)S(1)}, u32[]{:S(2)}, u32[]{:S(2)}) %collective-permute-start.1) | collective-permute-done | bytes 294944 | tf_op jit(solution)/shard_map/ppermute | solution.py:661
  12.6 1.3 %collective-permute-start.6 = (f32[9,96,128]{2,1,0:T(8,128)S(1)}, f32[9,96,128]{2,1,0:T(8,128)S(1)}, u32[]{:S(2)}, u32[]{:S(2)}) collective-permute-start(f32[9,96,128]{2,1,0:T(8,128)S(1)} %pack_relay.1), channel_id=1, source_target_pairs={{0,2},{2,4},{4,6},{6,8},{8,10},{10,12},{12,14},{14,16},{16,18},{18... | collective-permute-start | bytes 1327112 | tf_op jit(solution)/shard_map/ppermute | solution.py:655
  13.9 0.8 %apply_own.1 = (f32[2,2,2,96,128]{4,3,2,1,0:T(8,128)S(1)}, f32[2,2,96,128]{3,2,1,0:T(8,128)S(1)}, f32[2,2,96,128]{3,2,1,0:T(8,128)S(1)}, f32[2,2,96,128]{3,2,1,0:T(8,128)S(1)}, f32[2,2,2,96,128]{4,3,2,1,0:T(8,128)S(1)}) custom-call(f32[9,96,128]{2,1,0:T(8,128)S(1)} %pad_maximum_fusion.refs_0_.sources.refs_1_.eps, ...), custom_call_target="tpu_custom_call" | custom-call | bytes 1 | tf_op jit(solution)/shard_map/apply_own/pallas_call | solution.py:617
  14.7 1.1 %collective-permute-start.2 = (f32[2,2,96,128]{3,2,1,0:T(8,128)S(1)}, f32[2,2,96,128]{3,2,1,0:T(8,128)S(1)}, u32[]{:S(2)}, u32[]{:S(2)}) collective-permute-start(f32[2,2,96,128]{3,2,1,0:T(8,128)S(1)} %get-tuple-element.40), channel_id=1, source_target_pairs={{0,1},{1,0},{2,3},{3,2},{4,5},{5,4},{6,7},{7,6},{8,9},{9,8},{10,11... | collective-permute-start | bytes 589832 | tf_op jit(solution)/shard_map/ppermute | solution.py:658
  16.1 1.2 %collective-permute-done.4.refs_2_.refs_1_.refs_0_ = f32[9,96,128]{2,1,0:T(8,128)S(1)} collective-permute-done((f32[9,96,128]{2,1,0:T(8,128)S(1)}, f32[9,96,128]{2,1,0:T(8,128)S(1)}, u32[]{:S(2)}, u32[]{:S(2)}) %collective-permute-start.4) | collective-permute-done | bytes 442400 | tf_op jit(solution)/shard_map/ppermute | solution.py:655
  17.2 0.8 %apply_side.1 = (f32[2,2,2,96,128]{4,3,2,1,0:T(8,128)S(1)}, f32[2,2,96,128]{3,2,1,0:T(8,128)S(1)}, f32[2,2,2,96,128]{4,3,2,1,0:T(8,128)S(1)}) custom-call(f32[9,96,128]{2,1,0:T(8,128)S(1)} %pad_maximum_fusion.refs_0_.sources.refs_1_.eps, f32[6,96,128]{2,1,0:T(8,128)S(1)} %collective-permute-done.1.refs_2_.refs_1_.refs_0_.sources, ...), custom_call_target="tpu_custom_call" | custom-call | bytes 1 | tf_op jit(solution)/shard_map/apply_side/pallas_call | solution.py:617
  18.0 0.9 %apply_second.1 = (f32[2,2,2,96,128]{4,3,2,1,0:T(8,128)S(1)}, f32[2,2,96,128]{3,2,1,0:T(8,128)S(1)}, f32[2,2,2,96,128]{4,3,2,1,0:T(8,128)S(1)}) custom-call(f32[9,96,128]{2,1,0:T(8,128)S(1)} %pad_maximum_fusion.refs_0_.sources.refs_1_.eps, f32[2,2,2,96,128]{4,3,2,1,0:T(8,128)S(1)} %get-tuple-element.38.refs_1_.refs_2_, ...), custom_call_target="tpu_custom_call" | custom-call | bytes 1 | tf_op jit(solution)/shard_map/apply_second/pallas_call | solution.py:617
  18.9 0.5 products.1
  19.4 0.7 %collective-permute-start.5 = (f32[2,2,2,96,128]{4,3,2,1,0:T(8,128)S(1)}, f32[2,2,2,96,128]{4,3,2,1,0:T(8,128)S(1)}, u32[]{:S(2)}, u32[]{:S(2)}) collective-permute-start(f32[2,2,2,96,128]{4,3,2,1,0:T(8,128)S(1)} %get-tuple-element.48), channel_id=1, source_target_pairs={{0,1},{1,0},{2,3},{3,2},{4,5},{5,4},{6,7},{7,6},{8,9},{9,8},{10,11... | collective-permute-start | bytes 1179656 | tf_op jit(solution)/shard_map/ppermute | solution.py:658
  20.1 0.8 %apply_behind.1.refs_1_ = f32[2,2,2,96,128]{4,3,2,1,0:T(8,128)S(1)} custom-call(f32[6,96,128]{2,1,0:T(8,128)S(1)} %collective-permute-done.1.refs_2_.refs_1_.refs_0_.sources, f32[9,96,128]{2,1,0:T(8,128)S(1)} %collective-permute-done.4.refs_2_.refs_1_.refs_0_, f32[4,96,128]{2,1,0:T(8,128)S(1)} %get-tuple-element.35.refs_3_.refs_6_.refs_2_.refs_5_.refs_8_, ...), custom_call_target="tpu_custom_call" | custom-call | bytes 1 | tf_op jit(solution)/shard_map/apply_behind/pallas_call | solution.py:617
  20.9 0.8 %apply_side_second.1.refs_0_ = f32[2,2,2,96,128]{4,3,2,1,0:T(8,128)S(1)} custom-call(f32[9,96,128]{2,1,0:T(8,128)S(1)} %collective-permute-done.4.refs_2_.refs_1_.refs_0_, f32[2,2,2,96,128]{4,3,2,1,0:T(8,128)S(1)} %apply_behind.1.refs_1_, f32[2,2,2,96,128]{4,3,2,1,0:T(8,128)S(1)} %get-tuple-element.49.refs_2_, ...), custom_call_target="tpu_custom_call" | custom-call | bytes 1 | tf_op jit(solution)/shard_map/apply_side_second/pallas_call | solution.py:617
  22.0 0.3 add_far.1.refs_7_
  22.2 0.9 %apply_third.1 = f32[64,128]{1,0:T(8,128)S(1)} custom-call(f32[1,128]{1,0:T(1,128)S(1)} %get-tuple-element.47.refs_0_, f32[9,96,128]{2,1,0:T(8,128)S(1)} %pad_maximum_fusion.refs_0_.sources.refs_1_.eps, f32[2,2,2,96,128]{4,3,2,1,0:T(8,128)S(1)} %get-tuple-element.38.refs_1_.refs_2_, f32[2,2,96,128]{3,2,1,0:T(8,128)S(1)} %get-tuple-element.39.refs_2_.refs_3_, ...), custom_call_target="tpu_custom_call" | custom-call | bytes 1 | tf_op jit(solution)/shard_map/apply_third/pallas_call | solution.py:617
  23.2 22.0 %all_to_all.11 = f32[64,1,128]{2,1,0:T(1,128)S(1)} all-to-all(f32[64,1,128]{2,1,0:T(1,128)S(1)} %bitcast.13), channel_id=1, replica_groups=mesh['wl'=4,'gz'=64] {'gz'}, dimensions={0} | all-to-all | bytes 65536 | tf_op jit(solution)/shard_map/all_to_all | solution.py:758
  45.2 0.3 gradient.1
  45.4 2.8 %collective-permute-start.9 = (f32[24,128]{1,0:T(8,128)S(1)}, f32[24,128]{1,0:T(8,128)S(1)}, u32[]{:S(2)}, u32[]{:S(2)}) collective-permute-start(f32[24,128]{1,0:T(8,128)S(1)} %get-tuple-element.56), channel_id=1, source_target_pairs={{0,192},{64,0},{128,64},{192,128},{1,193},{65,1},{129,65},{193,129... | collective-permute-start | bytes 36872 | tf_op jit(solution)/shard_map/ppermute | solution.py:771
  48.2 0.3 collective-permute-start.8
  48.6 0.7 %collective-permute-start.7 = (f32[24,128]{1,0:T(8,128)S(1)}, f32[24,128]{1,0:T(8,128)S(1)}, u32[]{:S(2)}, u32[]{:S(2)}) collective-permute-start(f32[24,128]{1,0:T(8,128)S(1)} %get-tuple-element.54), channel_id=1, source_target_pairs={{0,64},{64,128},{128,192},{192,0},{1,65},{65,129},{129,193},{193,1... | collective-permute-start | bytes 36872 | tf_op jit(solution)/shard_map/ppermute | solution.py:771
  49.3 3.0 %collective-permute-done.8 = f32[24,128]{1,0:T(8,128)S(1)} collective-permute-done((f32[24,128]{1,0:T(8,128)S(1)}, f32[24,128]{1,0:T(8,128)S(1)}, u32[]{:S(2)}, u32[]{:S(2)}) %collective-permute-start.8) | collective-permute-done | bytes 12320 | tf_op jit(solution)/shard_map/ppermute | solution.py:771
  52.4 0.6 %add_bitcast_fusion = f32[1,24,128]{2,1,0:T(8,128)} fusion(f32[24,128]{1,0:T(8,128)S(1)} %collective-permute-done.9, f32[24,128]{1,0:T(8,128)S(1)} %collective-permute-done.8, f32[24,128]{1,0:T(8,128)S(1)} %get-tuple-element.53, f32[24,128]{1,0:T(8,128)S(1)} %collective-permute-done.7), kind=kLoop, calls=%fused_computation.1 | loop fusion | flops 9216 | bytes 61440 | tf_op jit(solution)/shard_map/broadcast_in_dim | solution.py:772
  (17 shorter events, 1.0 us)
Async XLA Ops:
  1.1 6.9 %collective-permute-start = (f32[9,96,128]{2,1,0:T(8,128)S(1)}, f32[9,96,128]{2,1,0:T(8,128)S(1)}, u32[]{:S(2)}, u32[]{:S(2)}) collective-permute-start(f32[9,96,128]{2,1,0:T(8,128)S(1)} %pad_maximum_fusion.refs_0_.sources.refs_1_.eps), channel_id=1, source_target_pairs={{0,1},{1,0},{2,3},{3,2},{4,5},{5,4},{6,7},{7,6},{8,9},{9,8},{10,11... | collective-permute-start | bytes 1327112 | tf_op jit(solution)/shard_map/ppermute | solution.py:658
  4.4 8.1 %collective-permute-start.1 = (f32[6,96,128]{2,1,0:T(8,128)S(1)}, f32[6,96,128]{2,1,0:T(8,128)S(1)}, u32[]{:S(2)}, u32[]{:S(2)}) collective-permute-start(f32[6,96,128]{2,1,0:T(8,128)S(1)} %slice.4), channel_id=1, source_target_pairs={{1,2},{2,1},{3,4},{4,3},{5,6},{6,5},{7,8},{8,7},{9,10},{10,9},{11,... | collective-permute-start | bytes 884744 | tf_op jit(solution)/shard_map/ppermute | solution.py:661
  6.4 0.7 %copy-start = (s32[3]{0:T(128)S(1)}, s32[3]{0:T(128)}, u32[]{:S(2)}) copy-start(s32[3]{0:T(128)} %param.10) | copy-start | bytes 40
  8.0 9.2 %collective-permute-start.4 = (f32[9,96,128]{2,1,0:T(8,128)S(1)}, f32[9,96,128]{2,1,0:T(8,128)S(1)}, u32[]{:S(2)}, u32[]{:S(2)}) collective-permute-start(f32[9,96,128]{2,1,0:T(8,128)S(1)} %pack.1), channel_id=1, source_target_pairs={{0,2},{2,4},{4,6},{6,8},{8,10},{10,12},{12,14},{14,16},{16,18},{18... | collective-permute-start | bytes 1327112 | tf_op jit(solution)/shard_map/ppermute | solution.py:655
  12.6 9.4 %collective-permute-start.6 = (f32[9,96,128]{2,1,0:T(8,128)S(1)}, f32[9,96,128]{2,1,0:T(8,128)S(1)}, u32[]{:S(2)}, u32[]{:S(2)}) collective-permute-start(f32[9,96,128]{2,1,0:T(8,128)S(1)} %pack_relay.1), channel_id=1, source_target_pairs={{0,2},{2,4},{4,6},{6,8},{8,10},{10,12},{12,14},{14,16},{16,18},{18... | collective-permute-start | bytes 1327112 | tf_op jit(solution)/shard_map/ppermute | solution.py:655
  14.7 3.3 %collective-permute-start.2 = (f32[2,2,96,128]{3,2,1,0:T(8,128)S(1)}, f32[2,2,96,128]{3,2,1,0:T(8,128)S(1)}, u32[]{:S(2)}, u32[]{:S(2)}) collective-permute-start(f32[2,2,96,128]{3,2,1,0:T(8,128)S(1)} %get-tuple-element.40), channel_id=1, source_target_pairs={{0,1},{1,0},{2,3},{3,2},{4,5},{5,4},{6,7},{7,6},{8,9},{9,8},{10,11... | collective-permute-start | bytes 589832 | tf_op jit(solution)/shard_map/ppermute | solution.py:658
  15.7 2.3 %collective-permute-start.3 = (f32[2,2,96,128]{3,2,1,0:T(8,128)S(1)}, f32[2,2,96,128]{3,2,1,0:T(8,128)S(1)}, u32[]{:S(2)}, u32[]{:S(2)}) collective-permute-start(f32[2,2,96,128]{3,2,1,0:T(8,128)S(1)} %get-tuple-element.41), channel_id=1, source_target_pairs={{0,1},{1,0},{2,3},{3,2},{4,5},{5,4},{6,7},{7,6},{8,9},{9,8},{10,11... | collective-permute-start | bytes 589832 | tf_op jit(solution)/shard_map/ppermute | solution.py:658
  19.4 2.8 %collective-permute-start.5 = (f32[2,2,2,96,128]{4,3,2,1,0:T(8,128)S(1)}, f32[2,2,2,96,128]{4,3,2,1,0:T(8,128)S(1)}, u32[]{:S(2)}, u32[]{:S(2)}) collective-permute-start(f32[2,2,2,96,128]{4,3,2,1,0:T(8,128)S(1)} %get-tuple-element.48), channel_id=1, source_target_pairs={{0,1},{1,0},{2,3},{3,2},{4,5},{5,4},{6,7},{7,6},{8,9},{9,8},{10,11... | collective-permute-start | bytes 1179656 | tf_op jit(solution)/shard_map/ppermute | solution.py:658
  45.4 3.9 %collective-permute-start.9 = (f32[24,128]{1,0:T(8,128)S(1)}, f32[24,128]{1,0:T(8,128)S(1)}, u32[]{:S(2)}, u32[]{:S(2)}) collective-permute-start(f32[24,128]{1,0:T(8,128)S(1)} %get-tuple-element.56), channel_id=1, source_target_pairs={{0,192},{64,0},{128,64},{192,128},{1,193},{65,1},{129,65},{193,129... | collective-permute-start | bytes 36872 | tf_op jit(solution)/shard_map/ppermute | solution.py:771
  48.2 4.1 %collective-permute-start.8 = (f32[24,128]{1,0:T(8,128)S(1)}, f32[24,128]{1,0:T(8,128)S(1)}, u32[]{:S(2)}, u32[]{:S(2)}) collective-permute-start(f32[24,128]{1,0:T(8,128)S(1)} %get-tuple-element.55), channel_id=1, source_target_pairs={{0,128},{64,192},{128,0},{192,64},{1,129},{65,193},{129,1},{193,65... | collective-permute-start | bytes 36872 | tf_op jit(solution)/shard_map/ppermute | solution.py:771
  48.6 3.8 %collective-permute-start.7 = (f32[24,128]{1,0:T(8,128)S(1)}, f32[24,128]{1,0:T(8,128)S(1)}, u32[]{:S(2)}, u32[]{:S(2)}) collective-permute-start(f32[24,128]{1,0:T(8,128)S(1)} %get-tuple-element.54), channel_id=1, source_target_pairs={{0,64},{64,128},{128,192},{192,0},{1,65},{65,129},{129,193},{193,1... | collective-permute-start | bytes 36872 | tf_op jit(solution)/shard_map/ppermute | solution.py:771

commit v5 on v4

--- a/solution.py
+++ b/solution.py
@@ -767,7 +767,7 @@
         name="gradient",
     )
     total = parts[0]
-    for k in range(1, shares):
+    for k in sorted(range(1, shares), key=lambda k: (-min(k, shares - k), k)):
         total = total + lax.ppermute(parts[k], "wl", [(i, (i + k) % shares) for i in range(shares)])
     return total[None]
 

time: 53.3 us -> 53.9 us (1.011); the launches traced: 53 us -> 53 us
  waiting for transfers between devices: 7.78 us -> 7.09 us
  starting transfers between devices: 13.6 us -> 14.2 us
    ppermute x3, waiting for transfers between devices: 3.14 us -> 2.45 us  [body(): lax.ppermute(parts[k], 'wl', [(i, (i + k) % shares) for i in range(shares)])]
    ppermute x3, starting transfers between devices: 3.85 us -> 4.46 us  [body(): lax.ppermute(parts[k], 'wl', [(i, (i + k) % shares) for i in range(shares)])]
where the time goes in v5:
time: 53.9 us; the launch traced here: 53 us
  blocking collectives  22 us (41%)
  starting transfers between devices  14.2 us (26%)
  waiting for transfers between devices  7.09 us (13%)
  Pallas kernels  6.36 us (12%)
  other arithmetic  1.69 us (3%)
  between operations  1.5 us (3%)
    all_to_all x1, blocking collectives, body(): rows = lax.all_to_all(rows, 'gz', 0, 0)  22 us
    pallas_call x13, Pallas kernels, call(): pl.pallas_call(kernel, out_shape=shapes, in_specs=specs, out_specs=outs_s...  6.36 us
    ppermute x4, starting transfers between devices, core_swap(): return lax.ppermute(value, 'gz', core_pairs)  5.23 us
    ppermute x3, starting transfers between devices, body(): lax.ppermute(parts[k], 'wl', [(i, (i + k) % shares) for i in range(shares)])  4.46 us
    ppermute x1, waiting for transfers between devices, body(): za = lax.ppermute(x[:6], 'gz', chip_pairs)  3.22 us
    ppermute x2, starting transfers between devices, behind(): return lax.ppermute(value, 'gz', behind_pairs)  2.58 us
    ppermute x3, waiting for transfers between devices, body(): lax.ppermute(parts[k], 'wl', [(i, (i + k) % shares) for i in range(shares)])  2.45 us
    ppermute x1, starting transfers between devices, body(): za = lax.ppermute(x[:6], 'gz', chip_pairs)  1.92 us
  transfers between devices with their start and end apart: 10, of which 5 were waited for; matrix products, arithmetic and copies ran while one was open for 0% of the time, Pallas kernels for 10%

profile of v5, /device:TPU:1, one launch (start us, length us, event | category | flops | bytes accessed | tf_op | source)
XLA Modules:
  0.0 53.0 jit_solution(8174765566136365547)
XLA Ops:
  0.0 1.1 %pad_maximum_fusion.refs_0_.sources.refs_1_.eps = f32[9,96,128]{2,1,0:T(8,128)S(1)} fusion(f32[3,96,128]{2,1,0:T(8,128)} %bitcast.16, f32[3,96,128]{2,1,0:T(8,128)} %bitcast.17, f32[3,96,128]{2,1,0:T(8,128)} %bitcast.18), kind=kLoop, calls=%fused_computation | loop fusion | flops 221184 | bytes 884736 | tf_op jit(solution)/shard_map/concatenate | solution.py:648
  1.1 3.3 %collective-permute-start = (f32[9,96,128]{2,1,0:T(8,128)S(1)}, f32[9,96,128]{2,1,0:T(8,128)S(1)}, u32[]{:S(2)}, u32[]{:S(2)}) collective-permute-start(f32[9,96,128]{2,1,0:T(8,128)S(1)} %pad_maximum_fusion.refs_0_.sources.refs_1_.eps), channel_id=1, source_target_pairs={{0,1},{1,0},{2,3},{3,2},{4,5},{5,4},{6,7},{7,6},{8,9},{9,8},{10,11... | collective-permute-start | bytes 1327112 | tf_op jit(solution)/shard_map/ppermute | solution.py:658
  4.4 1.9 %collective-permute-start.1 = (f32[6,96,128]{2,1,0:T(8,128)S(1)}, f32[6,96,128]{2,1,0:T(8,128)S(1)}, u32[]{:S(2)}, u32[]{:S(2)}) collective-permute-start(f32[6,96,128]{2,1,0:T(8,128)S(1)} %slice.4), channel_id=1, source_target_pairs={{1,2},{2,1},{3,4},{4,3},{5,6},{6,5},{7,8},{8,7},{9,10},{10,9},{11,... | collective-permute-start | bytes 884744 | tf_op jit(solution)/shard_map/ppermute | solution.py:661
  8.0 1.3 %collective-permute-start.4 = (f32[9,96,128]{2,1,0:T(8,128)S(1)}, f32[9,96,128]{2,1,0:T(8,128)S(1)}, u32[]{:S(2)}, u32[]{:S(2)}) collective-permute-start(f32[9,96,128]{2,1,0:T(8,128)S(1)} %pack.1), channel_id=1, source_target_pairs={{0,2},{2,4},{4,6},{6,8},{8,10},{10,12},{12,14},{14,16},{16,18},{18... | collective-permute-start | bytes 1327112 | tf_op jit(solution)/shard_map/ppermute | solution.py:655
  9.3 3.2 %collective-permute-done.1.refs_2_.refs_1_.refs_0_.sources = f32[6,96,128]{2,1,0:T(8,128)S(1)} collective-permute-done((f32[6,96,128]{2,1,0:T(8,128)S(1)}, f32[6,96,128]{2,1,0:T(8,128)S(1)}, u32[]{:S(2)}, u32[]{:S(2)}) %collective-permute-start.1) | collective-permute-done | bytes 294944 | tf_op jit(solution)/shard_map/ppermute | solution.py:661
  12.6 1.3 %collective-permute-start.6 = (f32[9,96,128]{2,1,0:T(8,128)S(1)}, f32[9,96,128]{2,1,0:T(8,128)S(1)}, u32[]{:S(2)}, u32[]{:S(2)}) collective-permute-start(f32[9,96,128]{2,1,0:T(8,128)S(1)} %pack_relay.1), channel_id=1, source_target_pairs={{0,2},{2,4},{4,6},{6,8},{8,10},{10,12},{12,14},{14,16},{16,18},{18... | collective-permute-start | bytes 1327112 | tf_op jit(solution)/shard_map/ppermute | solution.py:655
  13.9 0.8 %apply_own.1 = (f32[2,2,2,96,128]{4,3,2,1,0:T(8,128)S(1)}, f32[2,2,96,128]{3,2,1,0:T(8,128)S(1)}, f32[2,2,96,128]{3,2,1,0:T(8,128)S(1)}, f32[2,2,96,128]{3,2,1,0:T(8,128)S(1)}, f32[2,2,2,96,128]{4,3,2,1,0:T(8,128)S(1)}) custom-call(f32[9,96,128]{2,1,0:T(8,128)S(1)} %pad_maximum_fusion.refs_0_.sources.refs_1_.eps, ...), custom_call_target="tpu_custom_call" | custom-call | bytes 1 | tf_op jit(solution)/shard_map/apply_own/pallas_call | solution.py:617
  14.7 1.1 %collective-permute-start.2 = (f32[2,2,96,128]{3,2,1,0:T(8,128)S(1)}, f32[2,2,96,128]{3,2,1,0:T(8,128)S(1)}, u32[]{:S(2)}, u32[]{:S(2)}) collective-permute-start(f32[2,2,96,128]{3,2,1,0:T(8,128)S(1)} %get-tuple-element.40), channel_id=1, source_target_pairs={{0,1},{1,0},{2,3},{3,2},{4,5},{5,4},{6,7},{7,6},{8,9},{9,8},{10,11... | collective-permute-start | bytes 589832 | tf_op jit(solution)/shard_map/ppermute | solution.py:658
  16.1 1.2 %collective-permute-done.4.refs_2_.refs_1_.refs_0_ = f32[9,96,128]{2,1,0:T(8,128)S(1)} collective-permute-done((f32[9,96,128]{2,1,0:T(8,128)S(1)}, f32[9,96,128]{2,1,0:T(8,128)S(1)}, u32[]{:S(2)}, u32[]{:S(2)}) %collective-permute-start.4) | collective-permute-done | bytes 442400 | tf_op jit(solution)/shard_map/ppermute | solution.py:655
  17.2 0.8 %apply_side.1 = (f32[2,2,2,96,128]{4,3,2,1,0:T(8,128)S(1)}, f32[2,2,96,128]{3,2,1,0:T(8,128)S(1)}, f32[2,2,2,96,128]{4,3,2,1,0:T(8,128)S(1)}) custom-call(f32[9,96,128]{2,1,0:T(8,128)S(1)} %pad_maximum_fusion.refs_0_.sources.refs_1_.eps, f32[6,96,128]{2,1,0:T(8,128)S(1)} %collective-permute-done.1.refs_2_.refs_1_.refs_0_.sources, ...), custom_call_target="tpu_custom_call" | custom-call | bytes 1 | tf_op jit(solution)/shard_map/apply_side/pallas_call | solution.py:617
  18.0 0.9 %apply_second.1 = (f32[2,2,2,96,128]{4,3,2,1,0:T(8,128)S(1)}, f32[2,2,96,128]{3,2,1,0:T(8,128)S(1)}, f32[2,2,2,96,128]{4,3,2,1,0:T(8,128)S(1)}) custom-call(f32[9,96,128]{2,1,0:T(8,128)S(1)} %pad_maximum_fusion.refs_0_.sources.refs_1_.eps, f32[2,2,2,96,128]{4,3,2,1,0:T(8,128)S(1)} %get-tuple-element.38.refs_1_.refs_2_, ...), custom_call_target="tpu_custom_call" | custom-call | bytes 1 | tf_op jit(solution)/shard_map/apply_second/pallas_call | solution.py:617
  18.9 0.5 products.1
  19.4 0.7 %collective-permute-start.5 = (f32[2,2,2,96,128]{4,3,2,1,0:T(8,128)S(1)}, f32[2,2,2,96,128]{4,3,2,1,0:T(8,128)S(1)}, u32[]{:S(2)}, u32[]{:S(2)}) collective-permute-start(f32[2,2,2,96,128]{4,3,2,1,0:T(8,128)S(1)} %get-tuple-element.48), channel_id=1, source_target_pairs={{0,1},{1,0},{2,3},{3,2},{4,5},{5,4},{6,7},{7,6},{8,9},{9,8},{10,11... | collective-permute-start | bytes 1179656 | tf_op jit(solution)/shard_map/ppermute | solution.py:658
  20.1 0.8 %apply_behind.1.refs_1_ = f32[2,2,2,96,128]{4,3,2,1,0:T(8,128)S(1)} custom-call(f32[6,96,128]{2,1,0:T(8,128)S(1)} %collective-permute-done.1.refs_2_.refs_1_.refs_0_.sources, f32[9,96,128]{2,1,0:T(8,128)S(1)} %collective-permute-done.4.refs_2_.refs_1_.refs_0_, f32[4,96,128]{2,1,0:T(8,128)S(1)} %get-tuple-element.35.refs_3_.refs_6_.refs_2_.refs_5_.refs_8_, ...), custom_call_target="tpu_custom_call" | custom-call | bytes 1 | tf_op jit(solution)/shard_map/apply_behind/pallas_call | solution.py:617
  20.9 0.8 %apply_side_second.1.refs_0_ = f32[2,2,2,96,128]{4,3,2,1,0:T(8,128)S(1)} custom-call(f32[9,96,128]{2,1,0:T(8,128)S(1)} %collective-permute-done.4.refs_2_.refs_1_.refs_0_, f32[2,2,2,96,128]{4,3,2,1,0:T(8,128)S(1)} %apply_behind.1.refs_1_, f32[2,2,2,96,128]{4,3,2,1,0:T(8,128)S(1)} %get-tuple-element.49.refs_2_, ...), custom_call_target="tpu_custom_call" | custom-call | bytes 1 | tf_op jit(solution)/shard_map/apply_side_second/pallas_call | solution.py:617
  22.0 0.3 add_far.1.refs_7_
  22.2 0.9 %apply_third.1 = f32[64,128]{1,0:T(8,128)S(1)} custom-call(f32[1,128]{1,0:T(1,128)S(1)} %get-tuple-element.47.refs_0_, f32[9,96,128]{2,1,0:T(8,128)S(1)} %pad_maximum_fusion.refs_0_.sources.refs_1_.eps, f32[2,2,2,96,128]{4,3,2,1,0:T(8,128)S(1)} %get-tuple-element.38.refs_1_.refs_2_, f32[2,2,96,128]{3,2,1,0:T(8,128)S(1)} %get-tuple-element.39.refs_2_.refs_3_, ...), custom_call_target="tpu_custom_call" | custom-call | bytes 1 | tf_op jit(solution)/shard_map/apply_third/pallas_call | solution.py:617
  23.2 22.0 %all_to_all.11 = f32[64,1,128]{2,1,0:T(1,128)S(1)} all-to-all(f32[64,1,128]{2,1,0:T(1,128)S(1)} %bitcast.13), channel_id=1, replica_groups=mesh['wl'=4,'gz'=64] {'gz'}, dimensions={0} | all-to-all | bytes 65536 | tf_op jit(solution)/shard_map/all_to_all | solution.py:758
  45.2 0.3 gradient.1
  45.4 2.8 %collective-permute-start.9 = (f32[24,128]{1,0:T(8,128)S(1)}, f32[24,128]{1,0:T(8,128)S(1)}, u32[]{:S(2)}, u32[]{:S(2)}) collective-permute-start(f32[24,128]{1,0:T(8,128)S(1)} %get-tuple-element.56), channel_id=1, source_target_pairs={{0,192},{64,0},{128,64},{192,128},{1,193},{65,1},{129,65},{193,129... | collective-permute-start | bytes 36872 | tf_op jit(solution)/shard_map/ppermute | solution.py:771
  48.3 1.6 %collective-permute-start.7 = (f32[24,128]{1,0:T(8,128)S(1)}, f32[24,128]{1,0:T(8,128)S(1)}, u32[]{:S(2)}, u32[]{:S(2)}) collective-permute-start(f32[24,128]{1,0:T(8,128)S(1)} %get-tuple-element.54), channel_id=1, source_target_pairs={{0,128},{64,192},{128,0},{192,64},{1,129},{65,193},{129,1},{193,65... | collective-permute-start | bytes 36872 | tf_op jit(solution)/shard_map/ppermute | solution.py:771
  49.9 2.1 %collective-permute-done.8 = f32[24,128]{1,0:T(8,128)S(1)} collective-permute-done((f32[24,128]{1,0:T(8,128)S(1)}, f32[24,128]{1,0:T(8,128)S(1)}, u32[]{:S(2)}, u32[]{:S(2)}) %collective-permute-start.8) | collective-permute-done | bytes 12320 | tf_op jit(solution)/shard_map/ppermute | solution.py:771
  52.0 0.3 collective-permute-done.7
  52.4 0.6 %add_bitcast_fusion = f32[1,24,128]{2,1,0:T(8,128)} fusion(f32[24,128]{1,0:T(8,128)S(1)} %collective-permute-done.9, f32[24,128]{1,0:T(8,128)S(1)} %collective-permute-done.8, f32[24,128]{1,0:T(8,128)S(1)} %get-tuple-element.53, f32[24,128]{1,0:T(8,128)S(1)} %collective-permute-done.7), kind=kLoop, calls=%fused_computation.1 | loop fusion | flops 9216 | bytes 61440 | tf_op jit(solution)/shard_map/broadcast_in_dim | solution.py:772
  (17 shorter events, 0.9 us)
Async XLA Ops:
  1.1 6.9 %collective-permute-start = (f32[9,96,128]{2,1,0:T(8,128)S(1)}, f32[9,96,128]{2,1,0:T(8,128)S(1)}, u32[]{:S(2)}, u32[]{:S(2)}) collective-permute-start(f32[9,96,128]{2,1,0:T(8,128)S(1)} %pad_maximum_fusion.refs_0_.sources.refs_1_.eps), channel_id=1, source_target_pairs={{0,1},{1,0},{2,3},{3,2},{4,5},{5,4},{6,7},{7,6},{8,9},{9,8},{10,11... | collective-permute-start | bytes 1327112 | tf_op jit(solution)/shard_map/ppermute | solution.py:658
  4.4 8.1 %collective-permute-start.1 = (f32[6,96,128]{2,1,0:T(8,128)S(1)}, f32[6,96,128]{2,1,0:T(8,128)S(1)}, u32[]{:S(2)}, u32[]{:S(2)}) collective-permute-start(f32[6,96,128]{2,1,0:T(8,128)S(1)} %slice.4), channel_id=1, source_target_pairs={{1,2},{2,1},{3,4},{4,3},{5,6},{6,5},{7,8},{8,7},{9,10},{10,9},{11,... | collective-permute-start | bytes 884744 | tf_op jit(solution)/shard_map/ppermute | solution.py:661
  6.4 0.7 %copy-start = (s32[3]{0:T(128)S(1)}, s32[3]{0:T(128)}, u32[]{:S(2)}) copy-start(s32[3]{0:T(128)} %param.10) | copy-start | bytes 40
  8.0 9.2 %collective-permute-start.4 = (f32[9,96,128]{2,1,0:T(8,128)S(1)}, f32[9,96,128]{2,1,0:T(8,128)S(1)}, u32[]{:S(2)}, u32[]{:S(2)}) collective-permute-start(f32[9,96,128]{2,1,0:T(8,128)S(1)} %pack.1), channel_id=1, source_target_pairs={{0,2},{2,4},{4,6},{6,8},{8,10},{10,12},{12,14},{14,16},{16,18},{18... | collective-permute-start | bytes 1327112 | tf_op jit(solution)/shard_map/ppermute | solution.py:655
  12.6 9.4 %collective-permute-start.6 = (f32[9,96,128]{2,1,0:T(8,128)S(1)}, f32[9,96,128]{2,1,0:T(8,128)S(1)}, u32[]{:S(2)}, u32[]{:S(2)}) collective-permute-start(f32[9,96,128]{2,1,0:T(8,128)S(1)} %pack_relay.1), channel_id=1, source_target_pairs={{0,2},{2,4},{4,6},{6,8},{8,10},{10,12},{12,14},{14,16},{16,18},{18... | collective-permute-start | bytes 1327112 | tf_op jit(solution)/shard_map/ppermute | solution.py:655
  14.7 3.3 %collective-permute-start.2 = (f32[2,2,96,128]{3,2,1,0:T(8,128)S(1)}, f32[2,2,96,128]{3,2,1,0:T(8,128)S(1)}, u32[]{:S(2)}, u32[]{:S(2)}) collective-permute-start(f32[2,2,96,128]{3,2,1,0:T(8,128)S(1)} %get-tuple-element.40), channel_id=1, source_target_pairs={{0,1},{1,0},{2,3},{3,2},{4,5},{5,4},{6,7},{7,6},{8,9},{9,8},{10,11... | collective-permute-start | bytes 589832 | tf_op jit(solution)/shard_map/ppermute | solution.py:658
  15.7 2.3 %collective-permute-start.3 = (f32[2,2,96,128]{3,2,1,0:T(8,128)S(1)}, f32[2,2,96,128]{3,2,1,0:T(8,128)S(1)}, u32[]{:S(2)}, u32[]{:S(2)}) collective-permute-start(f32[2,2,96,128]{3,2,1,0:T(8,128)S(1)} %get-tuple-element.41), channel_id=1, source_target_pairs={{0,1},{1,0},{2,3},{3,2},{4,5},{5,4},{6,7},{7,6},{8,9},{9,8},{10,11... | collective-permute-start | bytes 589832 | tf_op jit(solution)/shard_map/ppermute | solution.py:658
  19.4 2.8 %collective-permute-start.5 = (f32[2,2,2,96,128]{4,3,2,1,0:T(8,128)S(1)}, f32[2,2,2,96,128]{4,3,2,1,0:T(8,128)S(1)}, u32[]{:S(2)}, u32[]{:S(2)}) collective-permute-start(f32[2,2,2,96,128]{4,3,2,1,0:T(8,128)S(1)} %get-tuple-element.48), channel_id=1, source_target_pairs={{0,1},{1,0},{2,3},{3,2},{4,5},{5,4},{6,7},{7,6},{8,9},{9,8},{10,11... | collective-permute-start | bytes 1179656 | tf_op jit(solution)/shard_map/ppermute | solution.py:658
  45.4 4.5 %collective-permute-start.9 = (f32[24,128]{1,0:T(8,128)S(1)}, f32[24,128]{1,0:T(8,128)S(1)}, u32[]{:S(2)}, u32[]{:S(2)}) collective-permute-start(f32[24,128]{1,0:T(8,128)S(1)} %get-tuple-element.56), channel_id=1, source_target_pairs={{0,192},{64,0},{128,64},{192,128},{1,193},{65,1},{129,65},{193,129... | collective-permute-start | bytes 36872 | tf_op jit(solution)/shard_map/ppermute | solution.py:771
  48.2 3.8 %collective-permute-start.8 = (f32[24,128]{1,0:T(8,128)S(1)}, f32[24,128]{1,0:T(8,128)S(1)}, u32[]{:S(2)}, u32[]{:S(2)}) collective-permute-start(f32[24,128]{1,0:T(8,128)S(1)} %get-tuple-element.55), channel_id=1, source_target_pairs={{0,64},{64,128},{128,192},{192,0},{1,65},{65,129},{129,193},{193,1... | collective-permute-start | bytes 36872 | tf_op jit(solution)/shard_map/ppermute | solution.py:771
  48.3 4.1 %collective-permute-start.7 = (f32[24,128]{1,0:T(8,128)S(1)}, f32[24,128]{1,0:T(8,128)S(1)}, u32[]{:S(2)}, u32[]{:S(2)}) collective-permute-start(f32[24,128]{1,0:T(8,128)S(1)} %get-tuple-element.54), channel_id=1, source_target_pairs={{0,128},{64,192},{128,0},{192,64},{1,129},{65,193},{129,1},{193,65... | collective-permute-start | bytes 36872 | tf_op jit(solution)/shard_map/ppermute | solution.py:771
